TPU v7x, 32 devices: a whole 2x2x4 slice. The times are simulated.
32 devices in a mesh: group: 2 (over y), tile: 8 (over z, x), strip: 2 (over core).
Axes of the slice: x: 2, y: 2, z: 4, core: 2. Of those that a mesh axis runs over, the one named last changes fastest.
Arguments:
- image: bfloat16 [128, 256, 256], P(('group', 'strip'), 'tile'), parts along dimension 0, may hold values from -16 to 16
- bn_gain: float32 [256], replicated, may hold values from 0.25 to 1.75
- bn_shift: float32 [256], replicated, may hold values from -3 to 3
- w_expand: bfloat16 [256, 1024], replicated, may hold values from -0.375 to 0.375
- b_expand: float32 [1024], replicated, may hold values from -3 to 3
- w_depth: float32 [9, 1024], replicated, may hold values from -2 to 2
- b_depth: float32 [1024], replicated, may hold values from -3 to 3
- w_project: bfloat16 [1024, 256], replicated, may hold values from -0.1875 to 0.1875
- b_project: float32 [256], replicated, may hold values from -3 to 3
- attn_gain: float32 [256], replicated, may hold values from 0.25 to 1.75
- attn_shift: float32 [256], replicated, may hold values from -2 to 2
- w_qkv: bfloat16 [256, 768], replicated, may hold values from -0.375 to 0.375
- w_out: bfloat16 [256, 256], replicated, may hold values from -0.375 to 0.375
- rel_table: float32 [8, 225], replicated, may hold values from -4 to 304
- ffn_gain: float32 [256], replicated, may hold values from 0.25 to 1.75
- ffn_shift: float32 [256], replicated, may hold values from -2 to 2
- w_up: bfloat16 [256, 1024], replicated, may hold values from -0.375 to 0.375
- b_up: float32 [1024], replicated, may hold values from -3 to 3
- w_down: bfloat16 [1024, 256], replicated, may hold values from -0.1875 to 0.1875
- b_down: float32 [256], replicated, may hold values from -3 to 3
Outputs:
- block_out: bfloat16 [128, 256, 256], P(('group', 'strip'), 'tile'), parts along dimension 0
There are 2 independent parts, one for each index of `group`. A program takes and returns all parts, laid end to end along the dimension named above; an argument that names none is the same for every part. Nothing has to cross between parts.
All inputs are finite; a program needn't handle non-finite values.
Results may differ from a plain program's by a relative error of at most 0.0064.
Values may be sent and summed in bfloat16 or wider, within the bound.
No kernel may reach another device: no remote copies, remote signals or barrier semaphores. Data moves between devices by JAX's collectives and lax.ppermute only.
A program may use at most 64 MiB of HBM per device.

v0:
```python
import functools

import jax
import jax.numpy as jnp
from jax import lax
from jax.experimental import pallas as pl
from jax.experimental.pallas import tpu as pltpu
from jax.sharding import PartitionSpec as P

GRID = 8
EPSILON = 1e-05
F32 = jnp.float32
BF16 = jnp.bfloat16
SLAB = 8
ROW_GAIN, ROW_SHIFT, ROW_EXPAND, ROW_DEPTH, ROW_PROJECT, ROW_TAPS, ROWS = 0, 1, 2, 3, 4, 8, 24
LANES = 128
VMEM_LIMIT = 48 * 1024 * 1024


def dot(lhs, rhs):
    return jnp.dot(lhs, rhs, preferred_element_type=F32)


def dot_nt(lhs, rhs):
    return lax.dot_general(lhs, rhs, (((1,), (1,)), ((), ())), preferred_element_type=F32)


def gelu(v):
    half = 0.5 * v
    inner = v * (0.7978845608028654 + (0.7978845608028654 * 0.044715) * (v * v))
    return half + half * jnp.tanh(inner)


def layer_norm(x, gain, shift):
    center = jnp.mean(x, axis=-1, keepdims=True)
    diff = x - center
    spread = jnp.mean(diff * diff, axis=-1, keepdims=True)
    return diff * lax.rsqrt(spread + EPSILON) * gain + shift


def full(shape):
    return pl.BlockSpec(shape, lambda *_: (0,) * len(shape))


VMEM = pl.BlockSpec(memory_space=pltpu.VMEM)
ANY = pl.BlockSpec(memory_space=pl.ANY)
PARAMS = pltpu.CompilerParams(vmem_limit_bytes=VMEM_LIMIT)


class Place:
    def __init__(self):
        self.strips = lax.axis_size("strip")
        self.tiles = lax.axis_size("tile")
        self.col_groups = self.tiles // GRID
        self.strip = lax.axis_index("strip")
        self.tile = lax.axis_index("tile")
        grid_col = self.tile // self.col_groups
        self.zi = grid_col // 2
        self.xc = (grid_col % 2) * self.strips + self.strip
        self.odd = self.tile % 2


def split3(x):
    high = x.astype(BF16)
    rest = x - high.astype(F32)
    middle = rest.astype(BF16)
    return [high, middle, (rest - middle.astype(F32)).astype(BF16)]


def edges_kernel(image_ref, beyond_ref, even_ref, odd_ref):
    place = Place()
    rows, cols, width = image_ref.shape
    pixels = image_ref[...].reshape(rows * cols, width)
    pick = lax.broadcasted_iota(jnp.int32, (2 * rows, rows * cols), 0)
    where = lax.broadcasted_iota(jnp.int32, (2 * rows, rows * cols), 1)
    first, last = place.odd, 1 - place.odd
    wanted = jnp.where(
        pick < rows, pick * cols + last * (cols - 1), (pick - rows) * cols + first * (cols - 1)
    )
    onehot = jnp.where(where == wanted, 1.0, 0.0).astype(BF16)
    columns = dot(onehot, pixels)
    beyond = beyond_ref[...].astype(F32)
    corners = [jnp.broadcast_to(beyond[c : c + 1], (2 * SLAB, width)) for c in (0, cols - 1)]
    for side, ref in ((0, even_ref), (1, odd_ref)):
        outer = place.odd == side
        corner = jnp.where(outer, corners[1], corners[0])
        ref[...] = jnp.concatenate([columns[side * rows : (side + 1) * rows], corner], axis=0).astype(BF16)


def edges(image, beyond):
    rows, cols, width = image.shape
    return pl.pallas_call(
        edges_kernel,
        out_shape=[jax.ShapeDtypeStruct((rows + 2 * SLAB, width), BF16)] * 2,
        compiler_params=PARAMS,
        cost_estimate=pl.CostEstimate(flops=4_000_000_000, bytes_accessed=1_000_000, transcendentals=0),
        name="edges",
    )(image, beyond)


def table_kernel(rel_ref, out_ref, rel_pad_ref, flat_ref):
    heads, entries = rel_ref.shape
    span = 2 * GRID - 1
    depth = rel_pad_ref.shape[1]
    rel_pad_ref[...] = jnp.zeros_like(rel_pad_ref)
    rel_pad_ref[:, :entries] = rel_ref[...]
    parts = jnp.concatenate(split3(rel_pad_ref[...]), axis=0)
    entry = lax.broadcasted_iota(jnp.int32, (depth, LANES), 0)
    lane = lax.broadcasted_iota(jnp.int32, (depth, LANES), 1)
    wanted = (lane % GRID + GRID - 1) * span + lane // GRID
    for k in range(GRID):
        onehot = jnp.where(entry == wanted - k * span, 1.0, 0.0).astype(BF16)
        found = dot(parts, onehot)
        flat_ref[k * heads : (k + 1) * heads, :] = (
            found[:heads] + found[heads : 2 * heads] + found[2 * heads :]
        )
    for h in range(heads):
        out_ref[h] = flat_ref[pl.ds(h, GRID, stride=heads), :]


def table(rel_table):
    heads, entries = rel_table.shape
    depth = -(-entries // LANES) * LANES
    return pl.pallas_call(
        table_kernel,
        out_shape=jax.ShapeDtypeStruct((heads, GRID, LANES), F32),
        scratch_shapes=[pltpu.VMEM((heads, depth), F32), pltpu.VMEM((GRID * heads, LANES), F32)],
        compiler_params=PARAMS,
        name="table",
    )(rel_table)


def expand_block(pixels, gain, shift, w_ref, bias, store):
    normed = (pixels.astype(F32) * gain + shift).astype(BF16)
    step = 2 * LANES
    for n in range(w_ref.shape[1] // step):
        part = slice(n * step, (n + 1) * step)
        store(part, gelu(dot(normed, w_ref[:, part]) + bias[:, part]))


def expand_kernel(image_ref, w_ref, *refs):
    out_ref, vectors_ref = refs[-2:]
    width, hidden = w_ref.shape
    vectors_ref[...] = jnp.zeros_like(vectors_ref)
    for line, ref in zip((ROW_GAIN, ROW_SHIFT, ROW_EXPAND, ROW_DEPTH, ROW_PROJECT, ROW_TAPS), refs):
        vectors_ref[line : line + ref.shape[0], : ref.shape[1]] = ref[...]
    rows, cols, _ = image_ref.shape
    per = SLAB
    gain = vectors_ref[ROW_GAIN : ROW_GAIN + 1, :width]
    shift = vectors_ref[ROW_SHIFT : ROW_SHIFT + 1, :width]
    bias = vectors_ref[ROW_EXPAND : ROW_EXPAND + 1, :]

    def step(i, carry):
        spot = pl.ds(i * per, per)

        def store(part, value):
            out_ref[spot, :, part] = value.astype(BF16).reshape(per, cols, value.shape[-1])

        expand_block(image_ref[spot].reshape(per * cols, width), gain, shift, w_ref, bias, store)
        return carry

    lax.fori_loop(0, rows // per, step, 0)


def expand(image, w_expand, vectors):
    rows, cols, width = image.shape
    hidden = w_expand.shape[1]
    return pl.pallas_call(
        expand_kernel,
        in_specs=[VMEM] * (2 + len(vectors)),
        out_specs=[VMEM] * 2,
        out_shape=[
            jax.ShapeDtypeStruct((rows, cols, hidden), BF16),
            jax.ShapeDtypeStruct((ROWS, hidden), F32),
        ],
        compiler_params=PARAMS,
        cost_estimate=pl.CostEstimate(
            flops=16 * rows * cols * width * hidden, bytes_accessed=4_000_000, transcendentals=rows * cols * hidden
        ),
        name="expand",
    )(image, w_expand, *vectors)


def conv_kernel(
    piece,
    expanded_ref,
    image_ref,
    even_ref,
    odd_ref,
    outer_ref,
    w_expand_ref,
    w_project_ref,
    vectors_ref,
    out0_ref,
    out1_ref,
    out2_ref,
    out3_ref,
    rim_ref,
    side_ref,
    beyond_ref,
    tap_ref,
    deep_ref,
):
    place = Place()
    rows, cols, width = image_ref.shape
    hidden = expanded_ref.shape[-1]
    places = 4
    groups = rows // SLAB
    first = piece * places
    zi, xc = place.zi, place.xc

    def tap(t):
        return vectors_ref[ROW_TAPS + t : ROW_TAPS + t + 1, :]

    is_odd = place.odd == 1
    even, odd = even_ref[...].astype(F32), odd_ref[...].astype(F32)
    left, right = jnp.where(is_odd, even, odd), jnp.where(is_odd, odd, even)
    rim_in = jnp.concatenate([left, right, outer_ref[...].astype(F32)], axis=0)

    def store(part, value):
        rim_ref[:, part] = value.astype(BF16).astype(F32)

    expand_block(
        rim_in,
        vectors_ref[ROW_GAIN : ROW_GAIN + 1, :width],
        vectors_ref[ROW_SHIFT : ROW_SHIFT + 1, :width],
        w_expand_ref,
        vectors_ref[ROW_EXPAND : ROW_EXPAND + 1, :],
        store,
    )
    ok_left, ok_right = place.tile > 0, place.tile < place.tiles - 1
    ok_up, ok_down = place.strip > 0, place.strip < place.strips - 1
    ok_outer = ok_up if piece == 0 else ok_down
    tall = rows + 2 * SLAB
    beyond_ref[...] = jnp.where(ok_outer, rim_ref[2 * tall : 2 * tall + cols, :], 0.0).astype(BF16)
    for side, ok in ((0, ok_left), (1, ok_right)):
        base = side * tall
        corner = rim_ref[base + rows : base + rows + 1, :]
        side_ref[1 : rows + 1, :] = jnp.where(ok, rim_ref[base : base + rows, :], 0.0)
        side_ref[0:1, :] = jnp.where(jnp.logical_and(ok, ok_up), corner, 0.0)
        side_ref[rows + 1 : rows + 2, :] = jnp.where(jnp.logical_and(ok, ok_down), corner, 0.0)
        j = 2 * side
        tap_ref[side] = (
            side_ref[0:rows, :] * tap(j)
            + side_ref[1 : rows + 1, :] * tap(3 + j)
            + side_ref[2 : rows + 2, :] * tap(6 + j)
        )

    col_id = lax.broadcasted_iota(jnp.int32, (cols, LANES), 0)

    def chunk(index, carry):
        lanes = pl.ds(pl.multiple_of(index * LANES, LANES), LANES)
        weights = [vectors_ref[ROW_TAPS + t : ROW_TAPS + t + 1, lanes] for t in range(9)]
        bias = vectors_ref[ROW_DEPTH : ROW_DEPTH + 1, lanes]
        for m in range(groups):
            above = m * SLAB + first - 1
            lines = []
            for q in range(places + 2):
                r = above + q
                if 0 <= r < rows:
                    lines.append(expanded_ref[r, :, lanes].astype(F32))
                else:
                    lines.append(beyond_ref[:, lanes].astype(F32))
            for q in range(places):
                r = above + 1 + q
                sums = [
                    lines[q] * weights[j] + lines[q + 1] * weights[3 + j] + lines[q + 2] * weights[6 + j]
                    for j in range(3)
                ]
                before = jnp.where(col_id == 0, tap_ref[0, r : r + 1, lanes], pltpu.roll(sums[0], 1, 0))
                after = jnp.where(
                    col_id == cols - 1, tap_ref[1, r : r + 1, lanes], pltpu.roll(sums[2], cols - 1, 0)
                )
                deep_ref[q, m, :, lanes] = gelu(before + sums[1] + after + bias).astype(BF16)
        return carry

    lax.fori_loop(0, hidden // LANES, chunk, 0)

    octets = cols // SLAB
    b_project = vectors_ref[ROW_PROJECT : ROW_PROJECT + 1, :width]
    for k, out_ref in enumerate((out0_ref, out1_ref, out2_ref, out3_ref)):
        q = jnp.bitwise_xor(zi, k)
        projected = dot(deep_ref[q].reshape(groups * cols, hidden), w_project_ref[...]) + b_project
        own = jnp.stack([image_ref[m * SLAB + first + q] for m in range(groups)]).astype(F32)
        section = (own + projected.reshape(groups, cols, width)).reshape(groups, octets, SLAB, width)
        for o in range(octets):
            out_ref[jnp.bitwise_xor(xc, o)] = section[:, o].reshape(groups * SLAB, width).astype(BF16)


def conv(piece, expanded, image, even, odd, outer, w_expand, w_project, vectors):
    rows, cols, width = image.shape
    hidden = expanded.shape[-1]
    groups = rows // SLAB
    tall = rows + 2 * SLAB
    shape = jax.ShapeDtypeStruct((4, groups * SLAB, width), BF16)
    return pl.pallas_call(
        functools.partial(conv_kernel, piece),
        in_specs=[VMEM] * 8,
        out_specs=[VMEM] * 4,
        out_shape=[shape] * 4,
        scratch_shapes=[
            pltpu.VMEM((2 * tall + cols, hidden), F32),
            pltpu.VMEM((rows + SLAB, hidden), F32),
            pltpu.VMEM((cols, hidden), BF16),
            pltpu.VMEM((2, rows, hidden), F32),
            pltpu.VMEM((4, groups, cols, hidden), BF16),
        ],
        compiler_params=PARAMS,
        cost_estimate=pl.CostEstimate(
            flops=rows * cols * width * hidden, bytes_accessed=6_000_000, transcendentals=rows * cols * hidden
        ),
        name="conv",
    )(expanded, image, even, odd, outer, w_expand, w_project, vectors)


def attend_kernel(
    heads,
    in0_ref,
    in1_ref,
    in2_ref,
    in3_ref,
    gain_ref,
    shift_ref,
    w_qkv_ref,
    w_out_ref,
    table_ref,
    out0_ref,
    out1_ref,
    out2_ref,
    out3_ref,
    token_ref,
    normed_ref,
    query_t_ref,
    value_t_ref,
    bias_ref,
):
    place = Place()
    zi, xc = place.zi, place.xc
    halves, count, _ = normed_ref.shape
    width = halves * LANES
    chunk_rows = token_ref.shape[1]
    head = width // heads
    tokens = GRID * GRID
    wins = count // tokens

    for j, ref in enumerate((in0_ref, in1_ref, in2_ref, in3_ref)):
        for k in range(4):
            slot = jnp.bitwise_xor(zi, k) * 4 + jnp.bitwise_xor(xc, j)
            x = ref[k].astype(F32)
            token_ref[slot] = x
            normed = layer_norm(x, gain_ref[...], shift_ref[...])
            spot = pl.ds(pl.multiple_of(slot * chunk_rows, chunk_rows), chunk_rows)
            for c in range(halves):
                normed_ref[c, spot, :] = normed[:, c * LANES : (c + 1) * LANES]

    query_t_ref[...] = w_qkv_ref[:, :width].T
    value_t_ref[...] = w_qkv_ref[:, 2 * width :].T
    left_half = lax.broadcasted_iota(jnp.int32, (tokens, 2 * tokens), 1) < tokens
    row_head = lax.broadcasted_iota(jnp.int32, (LANES, 2 * tokens), 0) // head
    per_group = LANES // head

    lane_half = lax.broadcasted_iota(jnp.int32, (GRID, 2 * tokens), 1) < tokens
    for h in range(heads):
        base = table_ref[h]
        for c in range(GRID):
            off = (GRID - 1 - c) * GRID
            one = pltpu.roll(base, (LANES - off) % LANES, 1)
            two = pltpu.roll(base, (LANES - off + tokens) % LANES, 1)
            bias_ref[h, c * GRID : (c + 1) * GRID, :] = jnp.where(lane_half, one, two)

    for pair in range(wins // 2):
        spots = [pl.ds(2 * pair + w, tokens, stride=wins) for w in range(2)]
        columns = [jnp.concatenate([normed_ref[c, s, :] for s in spots], axis=0) for c in range(halves)]
        normed = jnp.concatenate(columns, axis=1).astype(BF16)
        keys = dot(normed, w_qkv_ref[:, width : 2 * width]).astype(BF16)
        query_t = (dot_nt(query_t_ref[...], normed) * head ** (-0.5)).astype(BF16)
        value_t = dot_nt(value_t_ref[...], normed).astype(BF16)
        parts = []
        for h in range(heads):
            g = h // per_group
            span = slice(g * LANES, (g + 1) * LANES)
            own = jnp.where(row_head == h % per_group, query_t[span], jnp.zeros((), BF16))
            both = dot(keys[:, span], own)
            scores = jnp.where(left_half, both[:tokens], both[tokens:]) + bias_ref[h]
            weight = jnp.exp(scores - jnp.max(scores, axis=0, keepdims=True))
            probs = weight * (1.0 / jnp.sum(weight, axis=0, keepdims=True))
            spread = jnp.concatenate(
                [jnp.where(left_half, probs, 0.0), jnp.where(left_half, 0.0, probs)], axis=0
            ).astype(BF16)
            parts.append(dot(value_t[h * head : (h + 1) * head], spread))
        context = jnp.concatenate(parts, axis=0).astype(BF16).T
        attended = dot(context, w_out_ref[...])
        for w, spot in enumerate(spots):
            for c in range(halves):
                normed_ref[c, spot, :] = attended[w * tokens : (w + 1) * tokens, c * LANES : (c + 1) * LANES]

    for j, ref in enumerate((out0_ref, out1_ref, out2_ref, out3_ref)):
        for k in range(4):
            slot = jnp.bitwise_xor(zi, k) * 4 + jnp.bitwise_xor(xc, j)
            spot = pl.ds(pl.multiple_of(slot * chunk_rows, chunk_rows), chunk_rows)
            added = jnp.concatenate([normed_ref[c, spot, :] for c in range(halves)], axis=1)
            ref[k] = (token_ref[slot] + added).astype(BF16)


def attend(arrived, heads, weights):
    chunk_rows, width = arrived[0].shape[1:]
    count = 16 * chunk_rows
    flops = 2 * count * width * (4 * width)
    tokens = GRID * GRID
    shape = jax.ShapeDtypeStruct(arrived[0].shape, BF16)
    return pl.pallas_call(
        functools.partial(attend_kernel, heads),
        in_specs=[VMEM] * 9,
        out_specs=[VMEM] * 4,
        out_shape=[shape] * 4,
        scratch_shapes=[
            pltpu.VMEM((16, chunk_rows, width), F32),
            pltpu.VMEM((width // LANES, count, LANES), F32),
            pltpu.VMEM((width, width), BF16),
            pltpu.VMEM((width, width), BF16),
            pltpu.VMEM((heads, tokens, 2 * tokens), F32),
        ],
        compiler_params=PARAMS,
        cost_estimate=pl.CostEstimate(flops=flops, bytes_accessed=4_000_000, transcendentals=count * 512),
        name="attend",
    )(*arrived, *weights)


def feed_kernel(piece, *refs):
    in_refs = refs[:4]
    gain_ref, shift_ref, w_up_ref, b_up_ref, w_down_ref, b_down_ref = refs[4:10]
    out_ref, line_ref, sems = refs[-3:]
    place = Place()
    zi, xc = place.zi, place.xc
    groups, places, cols, width = line_ref.shape
    octets = cols // SLAB
    step = 2 * LANES
    for k, ref in enumerate(in_refs):
        slabs = [ref[jnp.bitwise_xor(xc, o)].astype(F32).reshape(groups, 1, SLAB, width) for o in range(octets)]
        section = jnp.concatenate(slabs, axis=1).reshape(groups * cols, width)
        normed = layer_norm(section, gain_ref[...], shift_ref[...]).astype(BF16)
        total = section + b_down_ref[...]
        for n in range(w_up_ref.shape[1] // step):
            inner = slice(n * step, (n + 1) * step)
            hidden = gelu(dot(normed, w_up_ref[:, inner]) + b_up_ref[:, inner]).astype(BF16)
            total = total + dot(hidden, w_down_ref[inner, :])
        result = total.reshape(groups, cols, width).astype(BF16)
        a = jnp.bitwise_xor(zi, k)
        for m in range(groups):
            line_ref[m, a] = result[m]
    copies = [
        pltpu.make_async_copy(
            line_ref.at[m], out_ref.at[pl.ds(m * SLAB + piece * places, places)], sems.at[m]
        )
        for m in range(groups)
    ]
    for copy in copies:
        copy.start()
    for copy in copies:
        copy.wait()


def feed(piece, sections, weights, image, partial):
    rows, cols, width = image.shape
    groups = rows // SLAB
    hidden = weights[2].shape[1]
    count = rows * cols // 2
    extra = [] if partial is None else [partial]
    return pl.pallas_call(
        functools.partial(feed_kernel, piece),
        in_specs=[VMEM] * 10 + [ANY] * len(extra),
        out_specs=ANY,
        out_shape=jax.ShapeDtypeStruct(image.shape, BF16),
        scratch_shapes=[pltpu.VMEM((groups, 4, cols, width), BF16), pltpu.SemaphoreType.DMA((groups,))],
        input_output_aliases={10: 0} if extra else {},
        compiler_params=PARAMS,
        cost_estimate=pl.CostEstimate(
            flops=4 * count * width * hidden, bytes_accessed=2_000_000, transcendentals=count * hidden
        ),
        name="feed",
    )(*sections, *weights, *extra)


def local(
    image,
    bn_gain,
    bn_shift,
    w_expand,
    b_expand,
    w_depth,
    b_depth,
    w_project,
    b_project,
    attn_gain,
    attn_shift,
    w_qkv,
    w_out,
    rel_table,
    ffn_gain,
    ffn_shift,
    w_up,
    b_up,
    w_down,
    b_down,
):
    rows, cols, width = image.shape
    strips = lax.axis_size("strip")
    tiles = lax.axis_size("tile")
    col_groups = tiles // GRID
    assert strips == 2 and rows * strips == GRID * SLAB and cols == 4 * SLAB
    strip = lax.axis_index("strip")

    def row(v):
        return v.reshape(1, -1)

    def exchange(value, mask):
        pairs = []
        for g in range(GRID):
            for c in range(col_groups):
                for s in range(strips):
                    member = (g * strips + s) ^ mask
                    source = (g * col_groups + c) * strips + s
                    target = ((member // strips) * col_groups + c) * strips + member % strips
                    pairs.append((source, target))
        return lax.ppermute(value, ("tile", "strip"), pairs)

    edge_row = lax.dynamic_index_in_dim(image, jnp.where(strip == 0, rows - 1, 0), 0, keepdims=False)
    beyond = lax.ppermute(edge_row, "strip", [(0, 1), (1, 0)])
    to_even, to_odd = edges(image, beyond)
    even_pairs = [(i, i ^ 1) for i in range(tiles)]
    odd_pairs = [(i, i + 1) for i in range(1, tiles - 1, 2)]
    odd_pairs = odd_pairs + [(j, i) for i, j in odd_pairs]
    even = lax.ppermute(to_even, "tile", even_pairs)
    odd = lax.ppermute(to_odd, "tile", odd_pairs)

    vectors_in = (row(bn_gain), row(bn_shift), row(b_expand), row(b_depth), row(b_project), w_depth)
    expanded, vectors = expand(image, w_expand, vectors_in)
    attend_weights = (row(attn_gain), row(attn_shift), w_qkv, w_out, table(rel_table))
    feed_weights = (row(ffn_gain), row(ffn_shift), w_up, row(b_up), w_down, row(b_down))
    heads = rel_table.shape[0]

    def sections_of(piece):
        return conv(piece, expanded, image, even, odd, beyond, w_expand, w_project, vectors)

    def along_z(blocks):
        return [blocks[0]] + [exchange(blocks[k], 4 * k) for k in range(1, 4)]

    def regroup(blocks):
        return [jnp.stack([blocks[k][j] for k in range(4)]) for j in range(4)]

    def within(blocks):
        return [blocks[0]] + [exchange(blocks[j], j) for j in range(1, 4)]

    def after(first, then):
        return lax.optimization_barrier((first, then))

    near_a = along_z(sections_of(0))
    sections_b = sections_of(1)
    near_a, sections_b = after(near_a, sections_b)
    held_a = within(regroup(near_a))
    held_a[1], sections_b = after(held_a[1], sections_b)
    near_b = along_z(sections_b)
    results_a = attend(held_a, heads, attend_weights)
    near_b, results_a = after(near_b, results_a)
    held_b = within(regroup(near_b))
    held_b[1], results_a = after(held_b[1], results_a)
    done_a = within(results_a)
    results_b = attend(held_b, heads, attend_weights)
    done_a, results_b = after(done_a, results_b)
    done_b = within(results_b)
    back_a = regroup(done_a)
    done_b[1], back_a = after(done_b[1], back_a)
    home_a = along_z(back_a)
    home_b = along_z(regroup(done_b))
    out = feed(0, home_a, feed_weights, image, None)
    return feed(1, home_b, feed_weights, image, out)


def solution(mesh):
    return jax.shard_map(
        local,
        mesh=mesh,
        in_specs=(P(("group", "strip"), "tile", None),) + (P(),) * 19,
        out_specs=P(("group", "strip"), "tile", None),
        check_vma=False,
    )
```

profile of v0, /device:TPU:0, one launch (start us, length us, event | category | flops | bytes accessed | tf_op | source)
XLA Modules:
  0.0 66.8 jit_solution(11151427222939226191)
XLA Ops:
  3.3 2.9 %collective-permute-start.1 = (bf16[48,256]{1,0:T(8,128)(2,1)S(1)}, bf16[48,256]{1,0:T(8,128)(2,1)S(1)}, u32[]{:S(2)}, u32[]{:S(2)}) collective-permute-start(bf16[48,256]{1,0:T(8,128)(2,1)S(1)} %get-tuple-element.65), channel_id=1, source_target_pairs={{0,2},{2,0},{4,6},{6,4},{8,10},{10,8},{12,14},{14,12},{1,3},{3,1},... | collective-permute-start | bytes 73736 | tf_op jit(solution)/shard_map/ppermute | solution.py:533
  7.0 2.0 %expand.1 = (bf16[32,32,1024]{2,1,0:T(8,128)(2,1)S(1)}, f32[24,1024]{1,0:T(8,128)S(1)}) custom-call(bf16[32,32,256]{2,1,0:T(8,128)(2,1)S(1)} %copy-done, bf16[256,1024]{1,0:T(8,128)(2,1)S(1)} %copy-done.2, f32[1,256]{1,0:T(1,128)S(1)} %bitcast.23, f32[1,256]{1,0:T(1,128)S(1)} %bitcast.24, f32[1,1024]{1,0:T(1,128)S(1)} %bitcast.21, f32[1,1024]{1,0:T(1,128)S(1)} %bitcast.22, ...), custom_call_target="tpu_custom_call" | custom-call | flops 4294967296 | bytes 4000000 | tf_op jit(solution)/shard_map/expand/pallas_call | solution.py:168
  9.1 3.3 %conv.2 = (bf16[4,32,256]{2,1,0:T(8,128)(2,1)S(1)}, bf16[4,32,256]{2,1,0:T(8,128)(2,1)S(1)}, bf16[4,32,256]{2,1,0:T(8,128)(2,1)S(1)}, bf16[4,32,256]{2,1,0:T(8,128)(2,1)S(1)}) custom-call(bf16[32,32,1024]{2,1,0:T(8,128)(2,1)S(1)} %get-tuple-element.64.expanded_ref, bf16[32,32,256]{2,1,0:T(8,128)(2,1)S(1)} %copy-done, ...), custom_call_target="tpu_custom_call" | custom-call | flops 268435456 | bytes 6000000 | tf_op jit(solution)/shard_map/conv/pallas_call | solution.py:296
  12.4 5.4 %collective-permute-start.3 = (bf16[4,32,256]{2,1,0:T(8,128)(2,1)S(1)}, bf16[4,32,256]{2,1,0:T(8,128)(2,1)S(1)}, u32[]{:S(2)}, u32[]{:S(2)}) collective-permute-start(bf16[4,32,256]{2,1,0:T(8,128)(2,1)S(1)} %get-tuple-element.69), channel_id=1, source_target_pairs={{0,4},{1,5},{2,6},{3,7},{4,0},{5,1},{6,2},{7,3},{8,12},{9,13},{10,... | collective-permute-start | bytes 196616 | tf_op jit(solution)/shard_map/ppermute | solution.py:525
  17.8 2.6 %collective-permute-start.4 = (bf16[4,32,256]{2,1,0:T(8,128)(2,1)S(1)}, bf16[4,32,256]{2,1,0:T(8,128)(2,1)S(1)}, u32[]{:S(2)}, u32[]{:S(2)}) collective-permute-start(bf16[4,32,256]{2,1,0:T(8,128)(2,1)S(1)} %get-tuple-element.70), channel_id=1, source_target_pairs={{0,8},{1,9},{2,10},{3,11},{4,12},{5,13},{6,14},{7,15},{8,0},{9,1},... | collective-permute-start | bytes 196616 | tf_op jit(solution)/shard_map/ppermute | solution.py:525
  20.7 3.3 %conv.3 = (bf16[4,32,256]{2,1,0:T(8,128)(2,1)S(1)}, bf16[4,32,256]{2,1,0:T(8,128)(2,1)S(1)}, bf16[4,32,256]{2,1,0:T(8,128)(2,1)S(1)}, bf16[4,32,256]{2,1,0:T(8,128)(2,1)S(1)}) custom-call(bf16[32,32,1024]{2,1,0:T(8,128)(2,1)S(1)} %get-tuple-element.64.expanded_ref, bf16[32,32,256]{2,1,0:T(8,128)(2,1)S(1)} %copy-done.1, ...), custom_call_target="tpu_custom_call" | custom-call | flops 268435456 | bytes 6000000 | tf_op jit(solution)/shard_map/conv/pallas_call | solution.py:296
  24.4 2.1 %collective-permute-done.5 = bf16[4,32,256]{2,1,0:T(8,128)(2,1)S(1)} collective-permute-done((bf16[4,32,256]{2,1,0:T(8,128)(2,1)S(1)}, bf16[4,32,256]{2,1,0:T(8,128)(2,1)S(1)}, u32[]{:S(2)}, u32[]{:S(2)}) %collective-permute-start.5) | collective-permute-done | bytes 65568 | tf_op jit(solution)/shard_map/ppermute | solution.py:525
  26.7 2.2 %collective-permute-start.10 = (bf16[4,32,256]{2,1,0:T(8,128)(2,1)S(1)}, bf16[4,32,256]{2,1,0:T(8,128)(2,1)S(1)}, u32[]{:S(2)}, u32[]{:S(2)}) collective-permute-start(bf16[4,32,256]{2,1,0:T(8,128)(2,1)S(1)} %pad_maximum_fusion.2), channel_id=1, source_target_pairs={{0,2},{1,3},{2,0},{3,1},{4,6},{5,7},{6,4},{7,5},{8,10},{9,11},{10,... | collective-permute-start | bytes 196616 | tf_op jit(solution)/shard_map/ppermute | solution.py:525
  28.9 2.0 %collective-permute-start.8 = (bf16[4,32,256]{2,1,0:T(8,128)(2,1)S(1)}, bf16[4,32,256]{2,1,0:T(8,128)(2,1)S(1)}, u32[]{:S(2)}, u32[]{:S(2)}) collective-permute-start(bf16[4,32,256]{2,1,0:T(8,128)(2,1)S(1)} %get-tuple-element.86), channel_id=1, source_target_pairs={{0,8},{1,9},{2,10},{3,11},{4,12},{5,13},{6,14},{7,15},{8,0},{9,1},... | collective-permute-start | bytes 196616 | tf_op jit(solution)/shard_map/ppermute | solution.py:525
  30.9 2.4 %collective-permute-start.9 = (bf16[4,32,256]{2,1,0:T(8,128)(2,1)S(1)}, bf16[4,32,256]{2,1,0:T(8,128)(2,1)S(1)}, u32[]{:S(2)}, u32[]{:S(2)}) collective-permute-start(bf16[4,32,256]{2,1,0:T(8,128)(2,1)S(1)} %get-tuple-element.87), channel_id=1, source_target_pairs={{0,12},{1,13},{2,14},{3,15},{4,8},{5,9},{6,10},{7,11},{8,4},{9,5},... | collective-permute-start | bytes 196616 | tf_op jit(solution)/shard_map/ppermute | solution.py:525
  33.3 3.1 %attend.2 = (bf16[4,32,256]{2,1,0:T(8,128)(2,1)S(1)}, bf16[4,32,256]{2,1,0:T(8,128)(2,1)S(1)}, bf16[4,32,256]{2,1,0:T(8,128)(2,1)S(1)}, bf16[4,32,256]{2,1,0:T(8,128)(2,1)S(1)}) custom-call(bf16[4,32,256]{2,1,0:T(8,128)(2,1)S(1)} %pad_maximum_fusion.1.in0_ref, bf16[4,32,256]{2,1,0:T(8,128)(2,1)S(1)} %collective-permute-done.6.in1_ref, ...), custom_call_target="tpu_custom_call" | custom-call | flops 268435456 | bytes 4000000 | tf_op jit(solution)/shard_map/attend/pallas_call | solution.py:411
  37.6 1.1 %collective-permute-start.12 = (bf16[4,32,256]{2,1,0:T(8,128)(2,1)S(1)}, bf16[4,32,256]{2,1,0:T(8,128)(2,1)S(1)}, u32[]{:S(2)}, u32[]{:S(2)}) collective-permute-start(bf16[4,32,256]{2,1,0:T(8,128)(2,1)S(1)} %pad_maximum_fusion.4), channel_id=1, source_target_pairs={{0,1},{1,0},{2,3},{3,2},{4,5},{5,4},{6,7},{7,6},{8,9},{9,8},{10,11... | collective-permute-start | bytes 196616 | tf_op jit(solution)/shard_map/ppermute | solution.py:525
  38.8 1.1 %collective-permute-start.16 = (bf16[4,32,256]{2,1,0:T(8,128)(2,1)S(1)}, bf16[4,32,256]{2,1,0:T(8,128)(2,1)S(1)}, u32[]{:S(2)}, u32[]{:S(2)}) collective-permute-start(bf16[4,32,256]{2,1,0:T(8,128)(2,1)S(1)} %pad_maximum_fusion.6), channel_id=1, source_target_pairs={{0,2},{1,3},{2,0},{3,1},{4,6},{5,7},{6,4},{7,5},{8,10},{9,11},{10,... | collective-permute-start | bytes 196616 | tf_op jit(solution)/shard_map/ppermute | solution.py:525
  41.8 1.4 %collective-permute-done.16.in2_ref = bf16[4,32,256]{2,1,0:T(8,128)(2,1)S(1)} collective-permute-done((bf16[4,32,256]{2,1,0:T(8,128)(2,1)S(1)}, bf16[4,32,256]{2,1,0:T(8,128)(2,1)S(1)}, u32[]{:S(2)}, u32[]{:S(2)}) %collective-permute-start.16) | collective-permute-done | bytes 65568 | tf_op jit(solution)/shard_map/ppermute | solution.py:525
  43.2 3.1 %attend.3 = (bf16[4,32,256]{2,1,0:T(8,128)(2,1)S(1)}, bf16[4,32,256]{2,1,0:T(8,128)(2,1)S(1)}, bf16[4,32,256]{2,1,0:T(8,128)(2,1)S(1)}, bf16[4,32,256]{2,1,0:T(8,128)(2,1)S(1)}) custom-call(bf16[4,32,256]{2,1,0:T(8,128)(2,1)S(1)} %pad_maximum_fusion.5.in0_ref, bf16[4,32,256]{2,1,0:T(8,128)(2,1)S(1)} %collective-permute-done.12.in1_ref, ...), custom_call_target="tpu_custom_call" | custom-call | flops 268435456 | bytes 4000000 | tf_op jit(solution)/shard_map/attend/pallas_call | solution.py:411
  46.5 1.3 %collective-permute-start.19 = (bf16[4,32,256]{2,1,0:T(8,128)(2,1)S(1)}, bf16[4,32,256]{2,1,0:T(8,128)(2,1)S(1)}, u32[]{:S(2)}, u32[]{:S(2)}) collective-permute-start(bf16[4,32,256]{2,1,0:T(8,128)(2,1)S(1)} %get-tuple-element.117), channel_id=1, source_target_pairs={{0,2},{1,3},{2,0},{3,1},{4,6},{5,7},{6,4},{7,5},{8,10},{9,11},{10,... | collective-permute-start | bytes 196616 | tf_op jit(solution)/shard_map/ppermute | solution.py:525
  48.4 1.6 %collective-permute-start.24 = (bf16[4,32,256]{2,1,0:T(8,128)(2,1)S(1)}, bf16[4,32,256]{2,1,0:T(8,128)(2,1)S(1)}, u32[]{:S(2)}, u32[]{:S(2)}) collective-permute-start(bf16[4,32,256]{2,1,0:T(8,128)(2,1)S(1)} %pad_maximum_fusion.9), channel_id=1, source_target_pairs={{0,4},{1,5},{2,6},{3,7},{4,0},{5,1},{6,2},{7,3},{8,12},{9,13},{10,... | collective-permute-start | bytes 196616 | tf_op jit(solution)/shard_map/ppermute | solution.py:525
  51.1 1.8 %collective-permute-start.26 = (bf16[4,32,256]{2,1,0:T(8,128)(2,1)S(1)}, bf16[4,32,256]{2,1,0:T(8,128)(2,1)S(1)}, u32[]{:S(2)}, u32[]{:S(2)}) collective-permute-start(bf16[4,32,256]{2,1,0:T(8,128)(2,1)S(1)} %pad_maximum_fusion.11), channel_id=1, source_target_pairs={{0,12},{1,13},{2,14},{3,15},{4,8},{5,9},{6,10},{7,11},{8,4},{9,5},... | collective-permute-start | bytes 196616 | tf_op jit(solution)/shard_map/ppermute | solution.py:525
  52.9 2.1 %collective-permute-start.23 = (bf16[4,32,256]{2,1,0:T(8,128)(2,1)S(1)}, bf16[4,32,256]{2,1,0:T(8,128)(2,1)S(1)}, u32[]{:S(2)}, u32[]{:S(2)}) collective-permute-start(bf16[4,32,256]{2,1,0:T(8,128)(2,1)S(1)} %pad_maximum_fusion.15), channel_id=1, source_target_pairs={{0,12},{1,13},{2,14},{3,15},{4,8},{5,9},{6,10},{7,11},{8,4},{9,5},... | collective-permute-start | bytes 196616 | tf_op jit(solution)/shard_map/ppermute | solution.py:525
  55.2 2.4 %collective-permute-start.21 = (bf16[4,32,256]{2,1,0:T(8,128)(2,1)S(1)}, bf16[4,32,256]{2,1,0:T(8,128)(2,1)S(1)}, u32[]{:S(2)}, u32[]{:S(2)}) collective-permute-start(bf16[4,32,256]{2,1,0:T(8,128)(2,1)S(1)} %pad_maximum_fusion.13), channel_id=1, source_target_pairs={{0,4},{1,5},{2,6},{3,7},{4,0},{5,1},{6,2},{7,3},{8,12},{9,13},{10,... | collective-permute-start | bytes 196616 | tf_op jit(solution)/shard_map/ppermute | solution.py:525
  57.6 3.5 %collective-permute-done.25.refs_2_ = bf16[4,32,256]{2,1,0:T(8,128)(2,1)S(1)} collective-permute-done((bf16[4,32,256]{2,1,0:T(8,128)(2,1)S(1)}, bf16[4,32,256]{2,1,0:T(8,128)(2,1)S(1)}, u32[]{:S(2)}, u32[]{:S(2)}) %collective-permute-start.25) | collective-permute-done | bytes 65568 | tf_op jit(solution)/shard_map/ppermute | solution.py:525
  61.1 2.0 %feed.2.refs_10_ = bf16[32,32,256]{2,1,0:T(8,128)(2,1)} custom-call(bf16[4,32,256]{2,1,0:T(8,128)(2,1)S(1)} %pad_maximum_fusion.8.refs_0_, bf16[4,32,256]{2,1,0:T(8,128)(2,1)S(1)} %collective-permute-done.24.refs_1_, bf16[4,32,256]{2,1,0:T(8,128)(2,1)S(1)} %collective-permute-done.25.refs_2_, bf16[4,32,256]{2,1,0:T(8,128)(2,1)S(1)} %collective-permute-done.26.refs_3_, ...), custom_call_target="tpu_custom_call" | custom-call | flops 536870912 | bytes 2000000 | tf_op jit(solution)/shard_map/feed/pallas_call | solution.py:469
  63.2 1.6 %collective-permute-done.22.refs_2_ = bf16[4,32,256]{2,1,0:T(8,128)(2,1)S(1)} collective-permute-done((bf16[4,32,256]{2,1,0:T(8,128)(2,1)S(1)}, bf16[4,32,256]{2,1,0:T(8,128)(2,1)S(1)}, u32[]{:S(2)}, u32[]{:S(2)}) %collective-permute-start.22) | collective-permute-done | bytes 65568 | tf_op jit(solution)/shard_map/ppermute | solution.py:525
  64.8 2.0 %feed.3 = bf16[32,32,256]{2,1,0:T(8,128)(2,1)} custom-call(bf16[4,32,256]{2,1,0:T(8,128)(2,1)S(1)} %pad_maximum_fusion.12.refs_0_, bf16[4,32,256]{2,1,0:T(8,128)(2,1)S(1)} %collective-permute-done.21.refs_1_, bf16[4,32,256]{2,1,0:T(8,128)(2,1)S(1)} %collective-permute-done.22.refs_2_, ...), custom_call_target="tpu_custom_call", output_to_operand_aliasing={{}: (10, {})} | custom-call | flops 536870912 | bytes 2000000 | tf_op jit(solution)/shard_map/feed/pallas_call | solution.py:469
  (112 shorter events, 9.9 us)
Async XLA Ops:
  3.3 5.7 %collective-permute-start.1 = (bf16[48,256]{1,0:T(8,128)(2,1)S(1)}, bf16[48,256]{1,0:T(8,128)(2,1)S(1)}, u32[]{:S(2)}, u32[]{:S(2)}) collective-permute-start(bf16[48,256]{1,0:T(8,128)(2,1)S(1)} %get-tuple-element.65), channel_id=1, source_target_pairs={{0,2},{2,0},{4,6},{6,4},{8,10},{10,8},{12,14},{14,12},{1,3},{3,1},... | collective-permute-start | bytes 73736 | tf_op jit(solution)/shard_map/ppermute | solution.py:533
  6.2 2.8 %collective-permute-start.2 = (bf16[48,256]{1,0:T(8,128)(2,1)S(1)}, bf16[48,256]{1,0:T(8,128)(2,1)S(1)}, u32[]{:S(2)}, u32[]{:S(2)}) collective-permute-start(bf16[48,256]{1,0:T(8,128)(2,1)S(1)} %get-tuple-element.66), channel_id=1, source_target_pairs={{2,4},{6,8},{10,12},{4,2},{8,6},{12,10},{3,5},{7,9},{11,13},{5,3},... | collective-permute-start | bytes 73736 | tf_op jit(solution)/shard_map/ppermute | solution.py:534
  12.4 11.7 %collective-permute-start.3 = (bf16[4,32,256]{2,1,0:T(8,128)(2,1)S(1)}, bf16[4,32,256]{2,1,0:T(8,128)(2,1)S(1)}, u32[]{:S(2)}, u32[]{:S(2)}) collective-permute-start(bf16[4,32,256]{2,1,0:T(8,128)(2,1)S(1)} %get-tuple-element.69), channel_id=1, source_target_pairs={{0,4},{1,5},{2,6},{3,7},{4,0},{5,1},{6,2},{7,3},{8,12},{9,13},{10,... | collective-permute-start | bytes 196616 | tf_op jit(solution)/shard_map/ppermute | solution.py:525
  17.8 6.6 %collective-permute-start.4 = (bf16[4,32,256]{2,1,0:T(8,128)(2,1)S(1)}, bf16[4,32,256]{2,1,0:T(8,128)(2,1)S(1)}, u32[]{:S(2)}, u32[]{:S(2)}) collective-permute-start(bf16[4,32,256]{2,1,0:T(8,128)(2,1)S(1)} %get-tuple-element.70), channel_id=1, source_target_pairs={{0,8},{1,9},{2,10},{3,11},{4,12},{5,13},{6,14},{7,15},{8,0},{9,1},... | collective-permute-start | bytes 196616 | tf_op jit(solution)/shard_map/ppermute | solution.py:525
  20.4 6.1 %collective-permute-start.5 = (bf16[4,32,256]{2,1,0:T(8,128)(2,1)S(1)}, bf16[4,32,256]{2,1,0:T(8,128)(2,1)S(1)}, u32[]{:S(2)}, u32[]{:S(2)}) collective-permute-start(bf16[4,32,256]{2,1,0:T(8,128)(2,1)S(1)} %get-tuple-element.71), channel_id=1, source_target_pairs={{0,12},{1,13},{2,14},{3,15},{4,8},{5,9},{6,10},{7,11},{8,4},{9,5},... | collective-permute-start | bytes 196616 | tf_op jit(solution)/shard_map/ppermute | solution.py:525
  26.5 6.8 %collective-permute-start.11 = (bf16[4,32,256]{2,1,0:T(8,128)(2,1)S(1)}, bf16[4,32,256]{2,1,0:T(8,128)(2,1)S(1)}, u32[]{:S(2)}, u32[]{:S(2)}) collective-permute-start(bf16[4,32,256]{2,1,0:T(8,128)(2,1)S(1)} %pad_maximum_fusion.3), channel_id=1, source_target_pairs={{0,3},{1,2},{2,1},{3,0},{4,7},{5,6},{6,5},{7,4},{8,11},{9,10},{10,... | collective-permute-start | bytes 196616 | tf_op jit(solution)/shard_map/ppermute | solution.py:525
  26.6 2.3 %collective-permute-start.6 = (bf16[4,32,256]{2,1,0:T(8,128)(2,1)S(1)}, bf16[4,32,256]{2,1,0:T(8,128)(2,1)S(1)}, u32[]{:S(2)}, u32[]{:S(2)}) collective-permute-start(bf16[4,32,256]{2,1,0:T(8,128)(2,1)S(1)} %pad_maximum_fusion), channel_id=1, source_target_pairs={{0,1},{1,0},{2,3},{3,2},{4,5},{5,4},{6,7},{7,6},{8,9},{9,8},{10,11... | collective-permute-start | bytes 196616 | tf_op jit(solution)/shard_map/ppermute | solution.py:525
  26.7 6.6 %collective-permute-start.10 = (bf16[4,32,256]{2,1,0:T(8,128)(2,1)S(1)}, bf16[4,32,256]{2,1,0:T(8,128)(2,1)S(1)}, u32[]{:S(2)}, u32[]{:S(2)}) collective-permute-start(bf16[4,32,256]{2,1,0:T(8,128)(2,1)S(1)} %pad_maximum_fusion.2), channel_id=1, source_target_pairs={{0,2},{1,3},{2,0},{3,1},{4,6},{5,7},{6,4},{7,5},{8,10},{9,11},{10,... | collective-permute-start | bytes 196616 | tf_op jit(solution)/shard_map/ppermute | solution.py:525
  28.9 7.6 %collective-permute-start.7 = (bf16[4,32,256]{2,1,0:T(8,128)(2,1)S(1)}, bf16[4,32,256]{2,1,0:T(8,128)(2,1)S(1)}, u32[]{:S(2)}, u32[]{:S(2)}) collective-permute-start(bf16[4,32,256]{2,1,0:T(8,128)(2,1)S(1)} %get-tuple-element.85), channel_id=1, source_target_pairs={{0,4},{1,5},{2,6},{3,7},{4,0},{5,1},{6,2},{7,3},{8,12},{9,13},{10,... | collective-permute-start | bytes 196616 | tf_op jit(solution)/shard_map/ppermute | solution.py:525
  28.9 8.5 %collective-permute-start.8 = (bf16[4,32,256]{2,1,0:T(8,128)(2,1)S(1)}, bf16[4,32,256]{2,1,0:T(8,128)(2,1)S(1)}, u32[]{:S(2)}, u32[]{:S(2)}) collective-permute-start(bf16[4,32,256]{2,1,0:T(8,128)(2,1)S(1)} %get-tuple-element.86), channel_id=1, source_target_pairs={{0,8},{1,9},{2,10},{3,11},{4,12},{5,13},{6,14},{7,15},{8,0},{9,1},... | collective-permute-start | bytes 196616 | tf_op jit(solution)/shard_map/ppermute | solution.py:525
  30.9 6.5 %collective-permute-start.9 = (bf16[4,32,256]{2,1,0:T(8,128)(2,1)S(1)}, bf16[4,32,256]{2,1,0:T(8,128)(2,1)S(1)}, u32[]{:S(2)}, u32[]{:S(2)}) collective-permute-start(bf16[4,32,256]{2,1,0:T(8,128)(2,1)S(1)} %get-tuple-element.87), channel_id=1, source_target_pairs={{0,12},{1,13},{2,14},{3,15},{4,8},{5,9},{6,10},{7,11},{8,4},{9,5},... | collective-permute-start | bytes 196616 | tf_op jit(solution)/shard_map/ppermute | solution.py:525
  37.5 4.3 %collective-permute-start.17 = (bf16[4,32,256]{2,1,0:T(8,128)(2,1)S(1)}, bf16[4,32,256]{2,1,0:T(8,128)(2,1)S(1)}, u32[]{:S(2)}, u32[]{:S(2)}) collective-permute-start(bf16[4,32,256]{2,1,0:T(8,128)(2,1)S(1)} %pad_maximum_fusion.7), channel_id=1, source_target_pairs={{0,3},{1,2},{2,1},{3,0},{4,7},{5,6},{6,5},{7,4},{8,11},{9,10},{10,... | collective-permute-start | bytes 196616 | tf_op jit(solution)/shard_map/ppermute | solution.py:525
  38.8 4.5 %collective-permute-start.16 = (bf16[4,32,256]{2,1,0:T(8,128)(2,1)S(1)}, bf16[4,32,256]{2,1,0:T(8,128)(2,1)S(1)}, u32[]{:S(2)}, u32[]{:S(2)}) collective-permute-start(bf16[4,32,256]{2,1,0:T(8,128)(2,1)S(1)} %pad_maximum_fusion.6), channel_id=1, source_target_pairs={{0,2},{1,3},{2,0},{3,1},{4,6},{5,7},{6,4},{7,5},{8,10},{9,11},{10,... | collective-permute-start | bytes 196616 | tf_op jit(solution)/shard_map/ppermute | solution.py:525
  39.9 6.4 %collective-permute-start.13 = (bf16[4,32,256]{2,1,0:T(8,128)(2,1)S(1)}, bf16[4,32,256]{2,1,0:T(8,128)(2,1)S(1)}, u32[]{:S(2)}, u32[]{:S(2)}) collective-permute-start(bf16[4,32,256]{2,1,0:T(8,128)(2,1)S(1)} %get-tuple-element.102), channel_id=1, source_target_pairs={{0,1},{1,0},{2,3},{3,2},{4,5},{5,4},{6,7},{7,6},{8,9},{9,8},{10,11... | collective-permute-start | bytes 196616 | tf_op jit(solution)/shard_map/ppermute | solution.py:525
  40.0 6.3 %collective-permute-start.14 = (bf16[4,32,256]{2,1,0:T(8,128)(2,1)S(1)}, bf16[4,32,256]{2,1,0:T(8,128)(2,1)S(1)}, u32[]{:S(2)}, u32[]{:S(2)}) collective-permute-start(bf16[4,32,256]{2,1,0:T(8,128)(2,1)S(1)} %get-tuple-element.103), channel_id=1, source_target_pairs={{0,2},{1,3},{2,0},{3,1},{4,6},{5,7},{6,4},{7,5},{8,10},{9,11},{10,... | collective-permute-start | bytes 196616 | tf_op jit(solution)/shard_map/ppermute | solution.py:525
  41.1 5.3 %collective-permute-start.15 = (bf16[4,32,256]{2,1,0:T(8,128)(2,1)S(1)}, bf16[4,32,256]{2,1,0:T(8,128)(2,1)S(1)}, u32[]{:S(2)}, u32[]{:S(2)}) collective-permute-start(bf16[4,32,256]{2,1,0:T(8,128)(2,1)S(1)} %get-tuple-element.104), channel_id=1, source_target_pairs={{0,3},{1,2},{2,1},{3,0},{4,7},{5,6},{6,5},{7,4},{8,11},{9,10},{10,... | collective-permute-start | bytes 196616 | tf_op jit(solution)/shard_map/ppermute | solution.py:525
  46.5 6.4 %collective-permute-start.19 = (bf16[4,32,256]{2,1,0:T(8,128)(2,1)S(1)}, bf16[4,32,256]{2,1,0:T(8,128)(2,1)S(1)}, u32[]{:S(2)}, u32[]{:S(2)}) collective-permute-start(bf16[4,32,256]{2,1,0:T(8,128)(2,1)S(1)} %get-tuple-element.117), channel_id=1, source_target_pairs={{0,2},{1,3},{2,0},{3,1},{4,6},{5,7},{6,4},{7,5},{8,10},{9,11},{10,... | collective-permute-start | bytes 196616 | tf_op jit(solution)/shard_map/ppermute | solution.py:525
  47.8 5.2 %collective-permute-start.20 = (bf16[4,32,256]{2,1,0:T(8,128)(2,1)S(1)}, bf16[4,32,256]{2,1,0:T(8,128)(2,1)S(1)}, u32[]{:S(2)}, u32[]{:S(2)}) collective-permute-start(bf16[4,32,256]{2,1,0:T(8,128)(2,1)S(1)} %get-tuple-element.118), channel_id=1, source_target_pairs={{0,3},{1,2},{2,1},{3,0},{4,7},{5,6},{6,5},{7,4},{8,11},{9,10},{10,... | collective-permute-start | bytes 196616 | tf_op jit(solution)/shard_map/ppermute | solution.py:525
  48.4 6.8 %collective-permute-start.24 = (bf16[4,32,256]{2,1,0:T(8,128)(2,1)S(1)}, bf16[4,32,256]{2,1,0:T(8,128)(2,1)S(1)}, u32[]{:S(2)}, u32[]{:S(2)}) collective-permute-start(bf16[4,32,256]{2,1,0:T(8,128)(2,1)S(1)} %pad_maximum_fusion.9), channel_id=1, source_target_pairs={{0,4},{1,5},{2,6},{3,7},{4,0},{5,1},{6,2},{7,3},{8,12},{9,13},{10,... | collective-permute-start | bytes 196616 | tf_op jit(solution)/shard_map/ppermute | solution.py:525
  50.0 11.1 %collective-permute-start.25 = (bf16[4,32,256]{2,1,0:T(8,128)(2,1)S(1)}, bf16[4,32,256]{2,1,0:T(8,128)(2,1)S(1)}, u32[]{:S(2)}, u32[]{:S(2)}) collective-permute-start(bf16[4,32,256]{2,1,0:T(8,128)(2,1)S(1)} %pad_maximum_fusion.10), channel_id=1, source_target_pairs={{0,8},{1,9},{2,10},{3,11},{4,12},{5,13},{6,14},{7,15},{8,0},{9,1},... | collective-permute-start | bytes 196616 | tf_op jit(solution)/shard_map/ppermute | solution.py:525
  51.1 10.0 %collective-permute-start.26 = (bf16[4,32,256]{2,1,0:T(8,128)(2,1)S(1)}, bf16[4,32,256]{2,1,0:T(8,128)(2,1)S(1)}, u32[]{:S(2)}, u32[]{:S(2)}) collective-permute-start(bf16[4,32,256]{2,1,0:T(8,128)(2,1)S(1)} %pad_maximum_fusion.11), channel_id=1, source_target_pairs={{0,12},{1,13},{2,14},{3,15},{4,8},{5,9},{6,10},{7,11},{8,4},{9,5},... | collective-permute-start | bytes 196616 | tf_op jit(solution)/shard_map/ppermute | solution.py:525
  52.9 10.2 %collective-permute-start.23 = (bf16[4,32,256]{2,1,0:T(8,128)(2,1)S(1)}, bf16[4,32,256]{2,1,0:T(8,128)(2,1)S(1)}, u32[]{:S(2)}, u32[]{:S(2)}) collective-permute-start(bf16[4,32,256]{2,1,0:T(8,128)(2,1)S(1)} %pad_maximum_fusion.15), channel_id=1, source_target_pairs={{0,12},{1,13},{2,14},{3,15},{4,8},{5,9},{6,10},{7,11},{8,4},{9,5},... | collective-permute-start | bytes 196616 | tf_op jit(solution)/shard_map/ppermute | solution.py:525
  55.1 9.7 %collective-permute-start.22 = (bf16[4,32,256]{2,1,0:T(8,128)(2,1)S(1)}, bf16[4,32,256]{2,1,0:T(8,128)(2,1)S(1)}, u32[]{:S(2)}, u32[]{:S(2)}) collective-permute-start(bf16[4,32,256]{2,1,0:T(8,128)(2,1)S(1)} %pad_maximum_fusion.14), channel_id=1, source_target_pairs={{0,8},{1,9},{2,10},{3,11},{4,12},{5,13},{6,14},{7,15},{8,0},{9,1},... | collective-permute-start | bytes 196616 | tf_op jit(solution)/shard_map/ppermute | solution.py:525
  55.2 9.6 %collective-permute-start.21 = (bf16[4,32,256]{2,1,0:T(8,128)(2,1)S(1)}, bf16[4,32,256]{2,1,0:T(8,128)(2,1)S(1)}, u32[]{:S(2)}, u32[]{:S(2)}) collective-permute-start(bf16[4,32,256]{2,1,0:T(8,128)(2,1)S(1)} %pad_maximum_fusion.13), channel_id=1, source_target_pairs={{0,4},{1,5},{2,6},{3,7},{4,0},{5,1},{6,2},{7,3},{8,12},{9,13},{10,... | collective-permute-start | bytes 196616 | tf_op jit(solution)/shard_map/ppermute | solution.py:525
  (24 other events, 266.7 us)
where the time goes:
time: 67.1 us; the launch traced here: 66.8 us
  starting transfers between devices  33.9 us (51%)
  Pallas kernels  19.3 us (29%)
  waiting for transfers between devices  10.7 us (16%)
  local copies, waits for them, and re-layouts  2.03 us (3%)
    ppermute x24, starting transfers between devices, exchange(): return lax.ppermute(value, ('tile', 'strip'), pairs)  29.9 us
    ppermute x24, waiting for transfers between devices, exchange(): return lax.ppermute(value, ('tile', 'strip'), pairs)  9.9 us
    pallas_call x2, Pallas kernels, conv(): pl.pallas_call(functools.partial(conv_kernel, piece), in_specs=[VMEM] * 8...  6.59 us
    pallas_call x2, Pallas kernels, attend(): pl.pallas_call(functools.partial(attend_kernel, heads), in_specs=[VMEM] *...  6.17 us
    pallas_call x2, Pallas kernels, feed(): pl.pallas_call(functools.partial(feed_kernel, piece), in_specs=[VMEM] * 1...  4.05 us
    ppermute x1, starting transfers between devices, local(): even = lax.ppermute(to_even, 'tile', even_pairs)  2.9 us
    pallas_call x1, Pallas kernels, expand(): pl.pallas_call(expand_kernel, in_specs=[VMEM] * (2 + len(vectors)), out_s...  2.02 us
  transfers between devices with their start and end apart: 27, of which 7 were waited for; matrix products, arithmetic and copies ran while one was open for 0% of the time, Pallas kernels for 21%

commit v1 on v0

v1 whole, which is shorter than its diff:
```python
import functools

import jax
import jax.numpy as jnp
from jax import lax
from jax.experimental import pallas as pl
from jax.experimental.pallas import tpu as pltpu
from jax.sharding import PartitionSpec as P

GRID = 8
EPSILON = 1e-05
F32 = jnp.float32
BF16 = jnp.bfloat16
SLAB = 8
ROW_GAIN, ROW_SHIFT, ROW_EXPAND, ROW_DEPTH, ROW_PROJECT, ROW_TAPS, ROWS = 0, 1, 2, 3, 4, 8, 24
LANES = 128
VMEM_LIMIT = 48 * 1024 * 1024


def dot(lhs, rhs):
    return jnp.dot(lhs, rhs, preferred_element_type=F32)


def dot_nt(lhs, rhs):
    return lax.dot_general(lhs, rhs, (((1,), (1,)), ((), ())), preferred_element_type=F32)


def gelu(v):
    half = 0.5 * v
    inner = v * (0.7978845608028654 + (0.7978845608028654 * 0.044715) * (v * v))
    return half + half * jnp.tanh(inner)


def layer_norm(x, gain, shift):
    center = jnp.mean(x, axis=-1, keepdims=True)
    diff = x - center
    spread = jnp.mean(diff * diff, axis=-1, keepdims=True)
    return diff * lax.rsqrt(spread + EPSILON) * gain + shift


def full(shape):
    return pl.BlockSpec(shape, lambda *_: (0,) * len(shape))


VMEM = pl.BlockSpec(memory_space=pltpu.VMEM)
ANY = pl.BlockSpec(memory_space=pl.ANY)
PARAMS = pltpu.CompilerParams(vmem_limit_bytes=VMEM_LIMIT)


class Place:
    def __init__(self):
        self.strips = lax.axis_size("strip")
        self.tiles = lax.axis_size("tile")
        self.col_groups = self.tiles // GRID
        self.strip = lax.axis_index("strip")
        self.tile = lax.axis_index("tile")
        grid_col = self.tile // self.col_groups
        self.zi = grid_col // 2
        self.xc = (grid_col % 2) * self.strips + self.strip
        self.odd = self.tile % 2


def split3(x):
    high = x.astype(BF16)
    rest = x - high.astype(F32)
    middle = rest.astype(BF16)
    return [high, middle, (rest - middle.astype(F32)).astype(BF16)]


def border_kernel(image_ref, out_ref):
    out_ref[...] = image_ref[jnp.where(Place().strip == 0, image_ref.shape[0] - 1, 0)]


def border(image):
    return pl.pallas_call(
        border_kernel,
        in_specs=[VMEM],
        out_specs=VMEM,
        out_shape=jax.ShapeDtypeStruct(image.shape[1:], BF16),
        compiler_params=PARAMS,
        name="border",
    )(image)


def edges_kernel(image_ref, beyond_ref, even_ref, odd_ref):
    place = Place()
    rows, cols, width = image_ref.shape
    pixels = image_ref[...].reshape(rows * cols, width)
    pick = lax.broadcasted_iota(jnp.int32, (2 * rows, rows * cols), 0)
    where = lax.broadcasted_iota(jnp.int32, (2 * rows, rows * cols), 1)
    first, last = place.odd, 1 - place.odd
    wanted = jnp.where(
        pick < rows, pick * cols + last * (cols - 1), (pick - rows) * cols + first * (cols - 1)
    )
    onehot = jnp.where(where == wanted, 1.0, 0.0).astype(BF16)
    columns = dot(onehot, pixels)
    beyond = beyond_ref[...].astype(F32)
    corners = [jnp.broadcast_to(beyond[c : c + 1], (2 * SLAB, width)) for c in (0, cols - 1)]
    for side, ref in ((0, even_ref), (1, odd_ref)):
        outer = place.odd == side
        corner = jnp.where(outer, corners[1], corners[0])
        ref[...] = jnp.concatenate([columns[side * rows : (side + 1) * rows], corner], axis=0).astype(BF16)


def edges(image, beyond):
    rows, cols, width = image.shape
    return pl.pallas_call(
        edges_kernel,
        out_shape=[jax.ShapeDtypeStruct((rows + 2 * SLAB, width), BF16)] * 2,
        compiler_params=PARAMS,
        cost_estimate=pl.CostEstimate(flops=4_000_000_000, bytes_accessed=1_000_000, transcendentals=0),
        name="edges",
    )(image, beyond)


def table_kernel(rel_ref, out_ref, rel_pad_ref, flat_ref):
    heads, entries = rel_ref.shape
    span = 2 * GRID - 1
    depth = rel_pad_ref.shape[1]
    rel_pad_ref[...] = jnp.zeros_like(rel_pad_ref)
    rel_pad_ref[:, :entries] = rel_ref[...]
    parts = jnp.concatenate(split3(rel_pad_ref[...]), axis=0)
    entry = lax.broadcasted_iota(jnp.int32, (depth, LANES), 0)
    lane = lax.broadcasted_iota(jnp.int32, (depth, LANES), 1)
    wanted = (lane % GRID + GRID - 1) * span + lane // GRID
    for k in range(GRID):
        onehot = jnp.where(entry == wanted - k * span, 1.0, 0.0).astype(BF16)
        found = dot(parts, onehot)
        flat_ref[k * heads : (k + 1) * heads, :] = (
            found[:heads] + found[heads : 2 * heads] + found[2 * heads :]
        )
    for h in range(heads):
        out_ref[h] = flat_ref[pl.ds(h, GRID, stride=heads), :]


def table(rel_table):
    heads, entries = rel_table.shape
    depth = -(-entries // LANES) * LANES
    return pl.pallas_call(
        table_kernel,
        out_shape=jax.ShapeDtypeStruct((heads, GRID, LANES), F32),
        scratch_shapes=[pltpu.VMEM((heads, depth), F32), pltpu.VMEM((GRID * heads, LANES), F32)],
        compiler_params=PARAMS,
        name="table",
    )(rel_table)


def expand_block(pixels, gain, shift, w_ref, bias, store):
    normed = (pixels.astype(F32) * gain + shift).astype(BF16)
    step = 2 * LANES
    for n in range(w_ref.shape[1] // step):
        part = slice(n * step, (n + 1) * step)
        store(part, gelu(dot(normed, w_ref[:, part]) + bias[:, part]))


def expand_kernel(image_ref, w_ref, *refs):
    out_ref, vectors_ref = refs[-2:]
    width, hidden = w_ref.shape
    vectors_ref[...] = jnp.zeros_like(vectors_ref)
    for line, ref in zip((ROW_GAIN, ROW_SHIFT, ROW_EXPAND, ROW_DEPTH, ROW_PROJECT, ROW_TAPS), refs):
        vectors_ref[line : line + ref.shape[0], : ref.shape[1]] = ref[...]
    rows, cols, _ = image_ref.shape
    gain = vectors_ref[ROW_GAIN : ROW_GAIN + 1, :width]
    shift = vectors_ref[ROW_SHIFT : ROW_SHIFT + 1, :width]

    def store(part, value):
        out_ref[:, :, part] = value.astype(BF16).reshape(rows, cols, value.shape[-1])

    pixels = image_ref[...].reshape(rows * cols, width)
    expand_block(pixels, gain, shift, w_ref, vectors_ref[ROW_EXPAND : ROW_EXPAND + 1, :], store)


def expand(image, w_expand, vectors):
    rows, cols, width = image.shape
    hidden = w_expand.shape[1]
    return pl.pallas_call(
        expand_kernel,
        in_specs=[VMEM] * (2 + len(vectors)),
        out_specs=[VMEM] * 2,
        out_shape=[
            jax.ShapeDtypeStruct((rows, cols, hidden), BF16),
            jax.ShapeDtypeStruct((ROWS, hidden), F32),
        ],
        compiler_params=PARAMS,
        cost_estimate=pl.CostEstimate(
            flops=16 * rows * cols * width * hidden, bytes_accessed=4_000_000, transcendentals=rows * cols * hidden
        ),
        name="expand",
    )(image, w_expand, *vectors)


def rim_kernel(even_ref, odd_ref, outer_ref, w_expand_ref, vectors_ref, tap_ref, beyond_ref, rim_ref, side_ref):
    place = Place()
    cols, width = outer_ref.shape
    rows = tap_ref.shape[1]

    def tap(t):
        return vectors_ref[ROW_TAPS + t : ROW_TAPS + t + 1, :]

    is_odd = place.odd == 1
    even, odd = even_ref[...].astype(F32), odd_ref[...].astype(F32)
    left, right = jnp.where(is_odd, even, odd), jnp.where(is_odd, odd, even)
    rim_in = jnp.concatenate([left, right, outer_ref[...].astype(F32)], axis=0)

    def store(part, value):
        rim_ref[:, part] = value.astype(BF16).astype(F32)

    expand_block(
        rim_in,
        vectors_ref[ROW_GAIN : ROW_GAIN + 1, :width],
        vectors_ref[ROW_SHIFT : ROW_SHIFT + 1, :width],
        w_expand_ref,
        vectors_ref[ROW_EXPAND : ROW_EXPAND + 1, :],
        store,
    )
    ok_up, ok_down = place.strip > 0, place.strip < place.strips - 1
    tall = rows + 2 * SLAB
    beyond_ref[...] = rim_ref[2 * tall : 2 * tall + cols, :].astype(BF16)
    for side, ok in ((0, place.tile > 0), (1, place.tile < place.tiles - 1)):
        base = side * tall
        corner = rim_ref[base + rows : base + rows + 1, :]
        side_ref[1 : rows + 1, :] = jnp.where(ok, rim_ref[base : base + rows, :], 0.0)
        side_ref[0:1, :] = jnp.where(jnp.logical_and(ok, ok_up), corner, 0.0)
        side_ref[rows + 1 : rows + 2, :] = jnp.where(jnp.logical_and(ok, ok_down), corner, 0.0)
        j = 2 * side
        tap_ref[side] = (
            side_ref[0:rows, :] * tap(j)
            + side_ref[1 : rows + 1, :] * tap(3 + j)
            + side_ref[2 : rows + 2, :] * tap(6 + j)
        )


def rim(rows, even, odd, outer, w_expand, vectors):
    hidden = w_expand.shape[1]
    cols = outer.shape[0]
    return pl.pallas_call(
        rim_kernel,
        in_specs=[VMEM] * 5,
        out_specs=[VMEM] * 2,
        out_shape=[
            jax.ShapeDtypeStruct((2, rows, hidden), F32),
            jax.ShapeDtypeStruct((cols, hidden), BF16),
        ],
        scratch_shapes=[
            pltpu.VMEM((2 * even.shape[0] + cols, hidden), F32),
            pltpu.VMEM((rows + SLAB, hidden), F32),
        ],
        compiler_params=PARAMS,
        cost_estimate=pl.CostEstimate(
            flops=2 * 4 * cols * outer.shape[1] * hidden, bytes_accessed=1_000_000, transcendentals=4 * cols * hidden
        ),
        name="rim",
    )(even, odd, outer, w_expand, vectors)


def conv_kernel(
    far,
    expanded_ref,
    image_ref,
    tap_ref,
    outer_ref,
    w_project_ref,
    vectors_ref,
    own_ref,
    core_ref,
    section_ref,
    deep_ref,
):
    place = Place()
    rows, cols, width = image_ref.shape
    hidden = expanded_ref.shape[-1]
    groups = rows // SLAB
    octets = cols // SLAB
    half = SLAB // 2
    zi, xc = place.zi, place.xc
    pair = jnp.bitwise_xor(zi // 2, far) * 2
    at_top = pair == 0
    ok_up, ok_down = place.strip > 0, place.strip < place.strips - 1
    slab_id = lax.broadcasted_iota(jnp.int32, (SLAB, LANES), 0)

    def chunk(index, carry):
        lanes = pl.ds(pl.multiple_of(index * LANES, LANES), LANES)
        weights = [vectors_ref[ROW_TAPS + t : ROW_TAPS + t + 1, lanes] for t in range(9)]
        bias = vectors_ref[ROW_DEPTH : ROW_DEPTH + 1, lanes]
        outer = outer_ref[:, lanes].astype(F32)
        above_all = jnp.where(ok_up, outer, 0.0)
        below_all = jnp.where(ok_down, outer, 0.0)
        for m in range(groups):
            for p in range(2):
                start = m * SLAB + p * half + pair
                lines = []
                for q in range(4):
                    r = start + q - 1
                    if m == 0 and p == 0 and q == 0:
                        inside = expanded_ref[jnp.maximum(r, 0), :, lanes].astype(F32)
                        lines.append(jnp.where(at_top, above_all, inside))
                    elif m == groups - 1 and p == 1 and q == 3:
                        inside = expanded_ref[jnp.minimum(r, rows - 1), :, lanes].astype(F32)
                        lines.append(jnp.where(at_top, inside, below_all))
                    else:
                        lines.append(expanded_ref[r, :, lanes].astype(F32))
                for i in range(2):
                    sums = [
                        lines[i] * weights[j] + lines[i + 1] * weights[3 + j] + lines[i + 2] * weights[6 + j]
                        for j in range(3)
                    ]
                    within = p * half + pair + i
                    left = pltpu.roll(tap_ref[0, m * SLAB : (m + 1) * SLAB, lanes], (SLAB - within) % SLAB, 0)
                    right = pltpu.roll(tap_ref[1, m * SLAB : (m + 1) * SLAB, lanes], SLAB - 1 - within, 0)
                    before, after = pltpu.roll(sums[0], 1, 0), pltpu.roll(sums[2], cols - 1, 0)
                    head = jnp.where(slab_id == 0, left, before[:SLAB])
                    tail = jnp.where(slab_id == SLAB - 1, right, after[-SLAB:])
                    before = jnp.concatenate([head, before[SLAB:]], axis=0)
                    after = jnp.concatenate([after[:-SLAB], tail], axis=0)
                    deep_ref[p, i, m, :, lanes] = gelu(before + sums[1] + after + bias).astype(BF16)
        return carry

    lax.fori_loop(0, hidden // LANES, chunk, 0)

    b_project = vectors_ref[ROW_PROJECT : ROW_PROJECT + 1, :width]
    for k in range(2):
        i = jnp.bitwise_xor(zi % 2, k)
        for p in range(2):
            projected = dot(deep_ref[p, i].reshape(groups * cols, hidden), w_project_ref[...]) + b_project
            own = jnp.stack([image_ref[m * SLAB + p * half + pair + i] for m in range(groups)]).astype(F32)
            section = (own + projected.reshape(groups, cols, width)).reshape(groups, octets, SLAB, width)
            for o in range(octets):
                section_ref[k, p, o] = section[:, o].reshape(groups * SLAB, width)
            for j in range(4):
                ref = core_ref if j % 2 else own_ref
                ref[k, j // 2, p] = section_ref[k, p, jnp.bitwise_xor(xc, j)].astype(BF16)


def conv(far, expanded, image, taps, outer, w_project, vectors):
    rows, cols, width = image.shape
    hidden = expanded.shape[-1]
    groups = rows // SLAB
    octets = cols // SLAB
    shape = jax.ShapeDtypeStruct((2, 2, 2, groups * SLAB, width), BF16)
    return pl.pallas_call(
        functools.partial(conv_kernel, far),
        in_specs=[VMEM] * 6,
        out_specs=[VMEM] * 2,
        out_shape=[shape] * 2,
        scratch_shapes=[
            pltpu.VMEM((2, 2, octets, groups * SLAB, width), F32),
            pltpu.VMEM((2, 2, groups, cols, hidden), BF16),
        ],
        compiler_params=PARAMS,
        cost_estimate=pl.CostEstimate(
            flops=rows * cols * width * hidden, bytes_accessed=6_000_000, transcendentals=rows * cols * hidden
        ),
        name="conv",
    )(expanded, image, taps, outer, w_project, vectors)


def attend_kernel(heads, *refs):
    in_refs, refs = refs[:8], refs[8:]
    gain_ref, shift_ref, w_qkv_ref, w_out_ref, table_ref, own_ref, core_ref = refs[:7]
    token_ref, normed_ref, query_t_ref, value_t_ref, bias_ref, window_ref, key_ref, qt_ref, vt_ref, context_ref = refs[7:]
    place = Place()
    zi, xc = place.zi, place.xc
    halves, count, _ = normed_ref.shape
    width = halves * LANES
    chunk_rows = token_ref.shape[2]
    head = width // heads
    tokens = GRID * GRID
    wins = chunk_rows // 4
    sources = tokens // 4

    def spot_of(p, slot):
        return pl.ds(pl.multiple_of((p * sources + slot) * chunk_rows, chunk_rows), chunk_rows)

    def slot_of(k, j):
        return jnp.bitwise_xor(zi, k) * 4 + jnp.bitwise_xor(xc, j)

    for k in range(4):
        for j in range(4):
            slot = slot_of(k, j)
            for p in range(2):
                x = in_refs[2 * k + j // 2][j % 2, p].astype(F32)
                token_ref[p, slot] = x
                normed = layer_norm(x, gain_ref[...], shift_ref[...])
                for c in range(halves):
                    normed_ref[c, spot_of(p, slot), :] = normed[:, c * LANES : (c + 1) * LANES]

    query_t_ref[...] = w_qkv_ref[:, :width].T
    value_t_ref[...] = w_qkv_ref[:, 2 * width :].T
    left_half = lax.broadcasted_iota(jnp.int32, (tokens, 2 * tokens), 1) < tokens
    row_head = lax.broadcasted_iota(jnp.int32, (LANES, 2 * tokens), 0) // head
    per_group = LANES // head

    lane_half = lax.broadcasted_iota(jnp.int32, (GRID, 2 * tokens), 1) < tokens
    for h in range(heads):
        base = table_ref[h]
        for c in range(GRID):
            off = (GRID - 1 - c) * GRID
            one = pltpu.roll(base, (LANES - off) % LANES, 1)
            two = pltpu.roll(base, (LANES - off + tokens) % LANES, 1)
            bias_ref[h, c * GRID : (c + 1) * GRID, :] = jnp.where(lane_half, one, two)

    def window(win):
        return pl.ds((win // wins) * tokens * wins + win % wins, tokens, stride=wins)

    for win in range(2 * wins):
        picked = [normed_ref[c, window(win), :] for c in range(halves)]
        window_ref[win * tokens : (win + 1) * tokens, :] = jnp.concatenate(picked, axis=1).astype(BF16)
    normed = window_ref[...]
    key_ref[...] = dot(normed, w_qkv_ref[:, width : 2 * width]).astype(BF16)
    qt_ref[...] = (dot_nt(query_t_ref[...], normed) * head ** (-0.5)).astype(BF16)
    vt_ref[...] = dot_nt(value_t_ref[...], normed).astype(BF16)

    for pair in range(wins):
        lanes = slice(pair * 2 * tokens, (pair + 1) * 2 * tokens)
        for h in range(heads):
            g = h // per_group
            span = slice(g * LANES, (g + 1) * LANES)
            own = jnp.where(row_head == h % per_group, qt_ref[span, lanes], jnp.zeros((), BF16))
            both = dot(key_ref[lanes, span], own)
            scores = jnp.where(left_half, both[:tokens], both[tokens:]) + bias_ref[h]
            weight = jnp.exp(scores - jnp.max(scores, axis=0, keepdims=True))
            probs = weight * (1.0 / jnp.sum(weight, axis=0, keepdims=True))
            spread = jnp.concatenate(
                [jnp.where(left_half, probs, 0.0), jnp.where(left_half, 0.0, probs)], axis=0
            ).astype(BF16)
            context_ref[h * head : (h + 1) * head, lanes] = dot(vt_ref[h * head : (h + 1) * head, lanes], spread)
    context = context_ref[...].T.astype(BF16)
    attended = dot(context, w_out_ref[...])
    for win in range(2 * wins):
        for c in range(halves):
            normed_ref[c, window(win), :] = attended[
                win * tokens : (win + 1) * tokens, c * LANES : (c + 1) * LANES
            ]

    for k in range(4):
        for j in range(4):
            slot = slot_of(k, j)
            ref = core_ref if j % 2 else own_ref
            for p in range(2):
                added = jnp.concatenate([normed_ref[c, spot_of(p, slot), :] for c in range(halves)], axis=1)
                ref[k, j // 2, p] = (token_ref[p, slot] + added).astype(BF16)


def attend(arrived, heads, weights):
    chunk_rows, width = arrived[0].shape[2:]
    count = 32 * chunk_rows
    flops = 2 * count * width * (4 * width)
    tokens = GRID * GRID
    shape = jax.ShapeDtypeStruct((4, 2, 2, chunk_rows, width), BF16)
    return pl.pallas_call(
        functools.partial(attend_kernel, heads),
        in_specs=[VMEM] * 13,
        out_specs=[VMEM] * 2,
        out_shape=[shape] * 2,
        scratch_shapes=[
            pltpu.VMEM((2, 16, chunk_rows, width), F32),
            pltpu.VMEM((width // LANES, count, LANES), F32),
            pltpu.VMEM((width, width), BF16),
            pltpu.VMEM((width, width), BF16),
            pltpu.VMEM((heads, tokens, 2 * tokens), F32),
            pltpu.VMEM((count, width), BF16),
            pltpu.VMEM((count, width), BF16),
            pltpu.VMEM((width, count), BF16),
            pltpu.VMEM((width, count), BF16),
            pltpu.VMEM((width, count), F32),
        ],
        compiler_params=PARAMS,
        cost_estimate=pl.CostEstimate(flops=flops, bytes_accessed=4_000_000, transcendentals=count * 512),
        name="attend",
    )(*arrived, *weights)


def feed_kernel(far, *refs):
    in_refs, refs = refs[:4], refs[4:]
    gain_ref, shift_ref, w_up_ref, b_up_ref, w_down_ref, b_down_ref = refs[:6]
    out_ref, line_ref, section_ref, sems = refs[-4:]
    place = Place()
    zi, xc = place.zi, place.xc
    groups, _, _, cols, width = line_ref.shape
    half = SLAB // 2
    pair = jnp.bitwise_xor(zi // 2, far) * 2
    step = 2 * LANES
    for k in range(2):
        i = jnp.bitwise_xor(zi % 2, k)
        for p in range(2):
            for j in range(4):
                o = jnp.bitwise_xor(xc, j)
                section_ref[k, p, o] = in_refs[2 * k + j // 2][j % 2, p].astype(F32)
            slabs = [section_ref[k, p, o].reshape(groups, 1, SLAB, width) for o in range(cols // SLAB)]
            section = jnp.concatenate(slabs, axis=1).reshape(groups * cols, width)
            normed = layer_norm(section, gain_ref[...], shift_ref[...]).astype(BF16)
            total = section + b_down_ref[...]
            for n in range(w_up_ref.shape[1] // step):
                inner = slice(n * step, (n + 1) * step)
                hidden = gelu(dot(normed, w_up_ref[:, inner]) + b_up_ref[:, inner]).astype(BF16)
                total = total + dot(hidden, w_down_ref[inner, :])
            result = total.reshape(groups, cols, width).astype(BF16)
            for m in range(groups):
                line_ref[m, p, i] = result[m]
    copies = [
        pltpu.make_async_copy(
            line_ref.at[m, p], out_ref.at[pl.ds(m * SLAB + p * half + pair, 2)], sems.at[2 * m + p]
        )
        for m in range(groups)
        for p in range(2)
    ]
    for copy in copies:
        copy.start()
    for copy in copies:
        copy.wait()


def feed(far, sections, weights, image, partial):
    rows, cols, width = image.shape
    groups = rows // SLAB
    hidden = weights[2].shape[1]
    count = rows * cols // 2
    extra = [] if partial is None else [partial]
    return pl.pallas_call(
        functools.partial(feed_kernel, far),
        in_specs=[VMEM] * 10 + [ANY] * len(extra),
        out_specs=ANY,
        out_shape=jax.ShapeDtypeStruct(image.shape, BF16),
        scratch_shapes=[
            pltpu.VMEM((groups, 2, 2, cols, width), BF16),
            pltpu.VMEM((2, 2, cols // SLAB, groups * SLAB, width), F32),
            pltpu.SemaphoreType.DMA((2 * groups,)),
        ],
        input_output_aliases={10: 0} if extra else {},
        compiler_params=PARAMS,
        cost_estimate=pl.CostEstimate(
            flops=4 * count * width * hidden, bytes_accessed=2_000_000, transcendentals=count * hidden
        ),
        name="feed",
    )(*sections, *weights, *extra)


def local(
    image,
    bn_gain,
    bn_shift,
    w_expand,
    b_expand,
    w_depth,
    b_depth,
    w_project,
    b_project,
    attn_gain,
    attn_shift,
    w_qkv,
    w_out,
    rel_table,
    ffn_gain,
    ffn_shift,
    w_up,
    b_up,
    w_down,
    b_down,
):
    rows, cols, width = image.shape
    strips = lax.axis_size("strip")
    tiles = lax.axis_size("tile")
    col_groups = tiles // GRID
    assert strips == 2 and rows * strips == GRID * SLAB and cols == 4 * SLAB

    def row(v):
        return v.reshape(1, -1)

    def exchange(value, mask):
        pairs = []
        for g in range(GRID):
            for c in range(col_groups):
                for s in range(strips):
                    member = (g * strips + s) ^ mask
                    source = (g * col_groups + c) * strips + s
                    target = ((member // strips) * col_groups + c) * strips + member % strips
                    pairs.append((source, target))
        return lax.ppermute(value, ("tile", "strip"), pairs)

    beyond = lax.ppermute(border(image), "strip", [(0, 1), (1, 0)])
    to_even, to_odd = edges(image, beyond)
    even_pairs = [(i, i ^ 1) for i in range(tiles)]
    odd_pairs = [(i, i + 1) for i in range(1, tiles - 1, 2)]
    odd_pairs = odd_pairs + [(j, i) for i, j in odd_pairs]
    odd = lax.ppermute(to_odd, "tile", odd_pairs)
    even = lax.ppermute(to_even, "tile", even_pairs)

    vectors_in = (row(bn_gain), row(bn_shift), row(b_expand), row(b_depth), row(b_project), w_depth)
    expanded, vectors = expand(image, w_expand, vectors_in)
    taps, outer = rim(rows, even, odd, beyond, w_expand, vectors)
    attend_weights = (row(attn_gain), row(attn_shift), w_qkv, w_out, table(rel_table))
    feed_weights = (row(ffn_gain), row(ffn_shift), w_up, row(b_up), w_down, row(b_down))
    heads = rel_table.shape[0]

    def after(first, then):
        return lax.optimization_barrier((first, then))

    def to_peer(outgoing, key):
        return exchange(outgoing[key], 4 * key[0] + 2 * key[1])

    far_keys = ((2, 0), (3, 0), (2, 1), (3, 1))
    near_keys = ((1, 0), (0, 1), (1, 1))

    def paired(own, from_core, first):
        return {
            (first + k, x): jnp.stack([own[k, x], from_core[k, x]]) for k in range(own.shape[0]) for x in range(2)
        }

    own, to_core = conv(0, expanded, image, taps, outer, w_project, vectors)
    outgoing = paired(own, exchange(to_core, 1), 0)
    arrived = {(0, 0): outgoing[0, 0]}
    arrived.update({key: to_peer(outgoing, key) for key in near_keys})
    own, to_core = conv(1, expanded, image, taps, outer, w_project, vectors)
    outgoing = paired(own, exchange(to_core, 1), 2)
    arrived.update({key: to_peer(outgoing, key) for key in far_keys})
    order = [(k, x) for k in range(4) for x in range(2)]
    own, to_core = attend([arrived[key] for key in order], heads, attend_weights)

    outgoing = paired(own, exchange(to_core, 1), 0)
    home = {(0, 0): outgoing[0, 0]}
    home.update({key: to_peer(outgoing, key) for key in near_keys})
    home[0, 1], outgoing = after(home[0, 1], outgoing)
    home.update({key: to_peer(outgoing, key) for key in far_keys})
    out = feed(0, [home[key] for key in order[:4]], feed_weights, image, None)
    return feed(1, [home[key] for key in order[4:]], feed_weights, image, out)


def solution(mesh):
    return jax.shard_map(
        local,
        mesh=mesh,
        in_specs=(P(("group", "strip"), "tile", None),) + (P(),) * 19,
        out_specs=P(("group", "strip"), "tile", None),
        check_vma=False,
    )
```

time: 67.1 us -> 61.6 us (0.918)
  Pallas kernels: 19.3 us -> 15.6 us
  local copies, waits for them, and re-layouts: 2.03 us -> 1.24 us
    pallas_call x2 -> x1, Pallas kernels: 6.17 us -> 2.77 us  [attend(): pl.pallas_call(functools.partial(attend_kernel, heads), in_specs=[VMEM] *...]
    squeeze x1 -> x0, local copies, waits for them, and re-layouts: 0.78 us -> none  [local(): lax.dynamic_index_in_dim(image, jnp.where(strip == 0, rows - 1, 0), 0, ke...]
    ppermute x24 -> x17, waiting for transfers between devices: 9.9 us -> 9.42 us  [exchange(): return lax.ppermute(value, ('tile', 'strip'), pairs)]
    ppermute x24 -> x17, starting transfers between devices: 29.9 us -> 29.7 us  [exchange(): return lax.ppermute(value, ('tile', 'strip'), pairs)]
    pallas_call x4 -> x6, Pallas kernels: 10.6 us -> 10.8 us  [the longest x2 6 us: conv(): pl.pallas_call(functools.partial(conv_kernel, far), in_specs=[VMEM] * 6,...]
  transfers between devices with their start and end apart: 27 -> 20, of which waited for: 7 -> 8; matrix products, arithmetic and copies ran while one was open for 0% -> 0% of each run, Pallas kernels for 21% -> 7%
where the time goes in v1:
time: 61.6 us; the launch traced here: 61.5 us
  starting transfers between devices  33.7 us (55%)
  Pallas kernels  15.6 us (25%)
  waiting for transfers between devices  10.3 us (17%)
  local copies, waits for them, and re-layouts  1.24 us (2%)
    ppermute x17, starting transfers between devices, exchange(): return lax.ppermute(value, ('tile', 'strip'), pairs)  29.7 us
    ppermute x17, waiting for transfers between devices, exchange(): return lax.ppermute(value, ('tile', 'strip'), pairs)  9.42 us
    pallas_call x2, Pallas kernels, conv(): pl.pallas_call(functools.partial(conv_kernel, far), in_specs=[VMEM] * 6,...  6 us
    pallas_call x2, Pallas kernels, feed(): pl.pallas_call(functools.partial(feed_kernel, far), in_specs=[VMEM] * 10...  4.26 us
    ppermute x1, starting transfers between devices, local(): even = lax.ppermute(to_even, 'tile', even_pairs)  2.9 us
    pallas_call x1, Pallas kernels, attend(): pl.pallas_call(functools.partial(attend_kernel, heads), in_specs=[VMEM] *...  2.77 us
    pallas_call x1, Pallas kernels, expand(): pl.pallas_call(expand_kernel, in_specs=[VMEM] * (2 + len(vectors)), out_s...  1.61 us
  transfers between devices with their start and end apart: 20, of which 8 were waited for; matrix products, arithmetic and copies ran while one was open for 0% of the time, Pallas kernels for 7%

profile of v1, /device:TPU:0, one launch (start us, length us, event | category | flops | bytes accessed | tf_op | source)
XLA Modules:
  0.0 61.5 jit_solution(16616159855942718095)
XLA Ops:
  0.0 1.0 %copy-done = bf16[32,32,256]{2,1,0:T(8,128)(2,1)S(1)} copy-done((bf16[32,32,256]{2,1,0:T(8,128)(2,1)S(1)}, bf16[32,32,256]{2,1,0:T(8,128)(2,1)}, u32[]{:S(2)}) %copy-start) | copy-done | bytes 524312
  2.7 2.9 %collective-permute-start.1 = (bf16[48,256]{1,0:T(8,128)(2,1)S(1)}, bf16[48,256]{1,0:T(8,128)(2,1)S(1)}, u32[]{:S(2)}, u32[]{:S(2)}) collective-permute-start(bf16[48,256]{1,0:T(8,128)(2,1)S(1)} %get-tuple-element.23), channel_id=1, source_target_pairs={{0,2},{2,0},{4,6},{6,4},{8,10},{10,8},{12,14},{14,12},{1,3},{3,1},... | collective-permute-start | bytes 73736 | tf_op jit(solution)/shard_map/ppermute | solution.py:586
  6.3 1.6 %expand.1 = (bf16[32,32,1024]{2,1,0:T(8,128)(2,1)S(1)}, f32[24,1024]{1,0:T(8,128)S(1)}) custom-call(bf16[32,32,256]{2,1,0:T(8,128)(2,1)S(1)} %copy-done, bf16[256,1024]{1,0:T(8,128)(2,1)S(1)} %copy-done.5, f32[1,256]{1,0:T(1,128)S(1)} %bitcast.85, f32[1,256]{1,0:T(1,128)S(1)} %bitcast.86, f32[1,1024]{1,0:T(1,128)S(1)} %bitcast.83, f32[1,1024]{1,0:T(1,128)S(1)} %bitcast.84, ...), custom_call_target="tpu_custom_call" | custom-call | flops 4294967296 | bytes 4000000 | tf_op jit(solution)/shard_map/expand/pallas_call | solution.py:176
  8.8 3.0 %conv.3 = (bf16[2,2,2,32,256]{4,3,2,1,0:T(8,128)(2,1)S(1)}, bf16[2,2,2,32,256]{4,3,2,1,0:T(8,128)(2,1)S(1)}) custom-call(bf16[32,32,1024]{2,1,0:T(8,128)(2,1)S(1)} %get-tuple-element.22.expanded_ref, bf16[32,32,256]{2,1,0:T(8,128)(2,1)S(1)} %copy-done.1, f32[2,32,1024]{2,1,0:T(8,128)S(1)} %get-tuple-element.26.tap_ref, ...), custom_call_target="tpu_custom_call" | custom-call | flops 268435456 | bytes 6000000 | tf_op jit(solution)/shard_map/conv/pallas_call | solution.py:340
  11.8 3.0 %conv.2 = (bf16[2,2,2,32,256]{4,3,2,1,0:T(8,128)(2,1)S(1)}, bf16[2,2,2,32,256]{4,3,2,1,0:T(8,128)(2,1)S(1)}) custom-call(bf16[32,32,1024]{2,1,0:T(8,128)(2,1)S(1)} %get-tuple-element.22.expanded_ref, bf16[32,32,256]{2,1,0:T(8,128)(2,1)S(1)} %copy-done.1, f32[2,32,1024]{2,1,0:T(8,128)S(1)} %get-tuple-element.26.tap_ref, ...), custom_call_target="tpu_custom_call" | custom-call | flops 268435456 | bytes 6000000 | tf_op jit(solution)/shard_map/conv/pallas_call | solution.py:340
  16.3 4.2 %collective-permute-start.11 = (bf16[2,2,32,256]{3,2,1,0:T(8,128)(2,1)S(1)}, bf16[2,2,32,256]{3,2,1,0:T(8,128)(2,1)S(1)}, u32[]{:S(2)}, u32[]{:S(2)}) collective-permute-start(bf16[2,2,32,256]{3,2,1,0:T(8,128)(2,1)S(1)} %pad_maximum_fusion.7), channel_id=1, source_target_pairs={{0,14},{1,15},{2,12},{3,13},{4,10},{5,11},{6,8},{7,9},{8,6},{9,7},... | collective-permute-start | bytes 196616 | tf_op jit(solution)/shard_map/ppermute | solution.py:578
  20.5 3.4 %collective-permute-start.10 = (bf16[2,2,32,256]{3,2,1,0:T(8,128)(2,1)S(1)}, bf16[2,2,32,256]{3,2,1,0:T(8,128)(2,1)S(1)}, u32[]{:S(2)}, u32[]{:S(2)}) collective-permute-start(bf16[2,2,32,256]{3,2,1,0:T(8,128)(2,1)S(1)} %pad_maximum_fusion.6), channel_id=1, source_target_pairs={{0,12},{1,13},{2,14},{3,15},{4,8},{5,9},{6,10},{7,11},{8,4},{9,5},... | collective-permute-start | bytes 196616 | tf_op jit(solution)/shard_map/ppermute | solution.py:578
  24.0 1.9 %collective-permute-start.9 = (bf16[2,2,32,256]{3,2,1,0:T(8,128)(2,1)S(1)}, bf16[2,2,32,256]{3,2,1,0:T(8,128)(2,1)S(1)}, u32[]{:S(2)}, u32[]{:S(2)}) collective-permute-start(bf16[2,2,32,256]{3,2,1,0:T(8,128)(2,1)S(1)} %pad_maximum_fusion.5), channel_id=1, source_target_pairs={{0,10},{1,11},{2,8},{3,9},{4,14},{5,15},{6,12},{7,13},{8,2},{9,3},... | collective-permute-start | bytes 196616 | tf_op jit(solution)/shard_map/ppermute | solution.py:578
  25.9 2.0 %collective-permute-start.8 = (bf16[2,2,32,256]{3,2,1,0:T(8,128)(2,1)S(1)}, bf16[2,2,32,256]{3,2,1,0:T(8,128)(2,1)S(1)}, u32[]{:S(2)}, u32[]{:S(2)}) collective-permute-start(bf16[2,2,32,256]{3,2,1,0:T(8,128)(2,1)S(1)} %pad_maximum_fusion.4), channel_id=1, source_target_pairs={{0,8},{1,9},{2,10},{3,11},{4,12},{5,13},{6,14},{7,15},{8,0},{9,1},... | collective-permute-start | bytes 196616 | tf_op jit(solution)/shard_map/ppermute | solution.py:578
  28.0 1.5 %collective-permute-start.6 = (bf16[2,2,32,256]{3,2,1,0:T(8,128)(2,1)S(1)}, bf16[2,2,32,256]{3,2,1,0:T(8,128)(2,1)S(1)}, u32[]{:S(2)}, u32[]{:S(2)}) collective-permute-start(bf16[2,2,32,256]{3,2,1,0:T(8,128)(2,1)S(1)} %pad_maximum_fusion.3), channel_id=1, source_target_pairs={{0,6},{1,7},{2,4},{3,5},{4,2},{5,3},{6,0},{7,1},{8,14},{9,15},{10,... | collective-permute-start | bytes 196616 | tf_op jit(solution)/shard_map/ppermute | solution.py:578
  30.2 2.2 %collective-permute-start.4 = (bf16[2,2,32,256]{3,2,1,0:T(8,128)(2,1)S(1)}, bf16[2,2,32,256]{3,2,1,0:T(8,128)(2,1)S(1)}, u32[]{:S(2)}, u32[]{:S(2)}) collective-permute-start(bf16[2,2,32,256]{3,2,1,0:T(8,128)(2,1)S(1)} %pad_maximum_fusion.1), channel_id=1, source_target_pairs={{0,2},{1,3},{2,0},{3,1},{4,6},{5,7},{6,4},{7,5},{8,10},{9,11},{10,... | collective-permute-start | bytes 196616 | tf_op jit(solution)/shard_map/ppermute | solution.py:578
  32.4 2.4 %collective-permute-done.9.refs_5_ = bf16[2,2,32,256]{3,2,1,0:T(8,128)(2,1)S(1)} collective-permute-done((bf16[2,2,32,256]{3,2,1,0:T(8,128)(2,1)S(1)}, bf16[2,2,32,256]{3,2,1,0:T(8,128)(2,1)S(1)}, u32[]{:S(2)}, u32[]{:S(2)}) %collective-permute-start.9) | collective-permute-done | bytes 65568 | tf_op jit(solution)/shard_map/ppermute | solution.py:578
  35.8 2.8 %attend.1 = (bf16[4,2,2,32,256]{4,3,2,1,0:T(8,128)(2,1)S(1)}, bf16[4,2,2,32,256]{4,3,2,1,0:T(8,128)(2,1)S(1)}) custom-call(bf16[2,2,32,256]{3,2,1,0:T(8,128)(2,1)S(1)} %pad_maximum_fusion.refs_0_, bf16[2,2,32,256]{3,2,1,0:T(8,128)(2,1)S(1)} %collective-permute-done.4.refs_1_, bf16[2,2,32,256]{3,2,1,0:T(8,128)(2,1)S(1)} %collective-permute-done.5.refs_2_, ...), custom_call_target="tpu_custom_call" | custom-call | flops 536870912 | bytes 4000000 | tf_op jit(solution)/shard_map/attend/pallas_call | solution.py:450
  38.7 1.5 %collective-permute-done.12 = bf16[4,2,2,32,256]{4,3,2,1,0:T(8,128)(2,1)S(1)} collective-permute-done((bf16[4,2,2,32,256]{4,3,2,1,0:T(8,128)(2,1)S(1)}, bf16[4,2,2,32,256]{4,3,2,1,0:T(8,128)(2,1)S(1)}, u32[]{:S(2)}, u32[]{:S(2)}) %collective-permute-start.12) | collective-permute-done | bytes 262176 | tf_op jit(solution)/shard_map/ppermute | solution.py:578
  40.3 0.9 %collective-permute-start.13 = (bf16[2,2,32,256]{3,2,1,0:T(8,128)(2,1)S(1)}, bf16[2,2,32,256]{3,2,1,0:T(8,128)(2,1)S(1)}, u32[]{:S(2)}, u32[]{:S(2)}) collective-permute-start(bf16[2,2,32,256]{3,2,1,0:T(8,128)(2,1)S(1)} %pad_maximum_fusion.8), channel_id=1, source_target_pairs={{0,2},{1,3},{2,0},{3,1},{4,6},{5,7},{6,4},{7,5},{8,10},{9,11},{10,... | collective-permute-start | bytes 196616 | tf_op jit(solution)/shard_map/ppermute | solution.py:578
  41.2 1.5 %collective-permute-start.19 = (bf16[2,2,32,256]{3,2,1,0:T(8,128)(2,1)S(1)}, bf16[2,2,32,256]{3,2,1,0:T(8,128)(2,1)S(1)}, u32[]{:S(2)}, u32[]{:S(2)}) collective-permute-start(bf16[2,2,32,256]{3,2,1,0:T(8,128)(2,1)S(1)} %pad_maximum_fusion.11), channel_id=1, source_target_pairs={{0,6},{1,7},{2,4},{3,5},{4,2},{5,3},{6,0},{7,1},{8,14},{9,15},{10,... | collective-permute-start | bytes 196616 | tf_op jit(solution)/shard_map/ppermute | solution.py:578
  42.7 1.3 %collective-permute-start.18 = (bf16[2,2,32,256]{3,2,1,0:T(8,128)(2,1)S(1)}, bf16[2,2,32,256]{3,2,1,0:T(8,128)(2,1)S(1)}, u32[]{:S(2)}, u32[]{:S(2)}) collective-permute-start(bf16[2,2,32,256]{3,2,1,0:T(8,128)(2,1)S(1)} %pad_maximum_fusion.10), channel_id=1, source_target_pairs={{0,4},{1,5},{2,6},{3,7},{4,0},{5,1},{6,2},{7,3},{8,12},{9,13},{10,... | collective-permute-start | bytes 196616 | tf_op jit(solution)/shard_map/ppermute | solution.py:578
  44.6 3.7 %collective-permute-start.14 = (bf16[2,2,32,256]{3,2,1,0:T(8,128)(2,1)S(1)}, bf16[2,2,32,256]{3,2,1,0:T(8,128)(2,1)S(1)}, u32[]{:S(2)}, u32[]{:S(2)}) collective-permute-start(bf16[2,2,32,256]{3,2,1,0:T(8,128)(2,1)S(1)} %get-tuple-element.34), channel_id=1, source_target_pairs={{0,8},{1,9},{2,10},{3,11},{4,12},{5,13},{6,14},{7,15},{8,0},{9,1},... | collective-permute-start | bytes 196616 | tf_op jit(solution)/shard_map/ppermute | solution.py:578
  48.3 1.9 %collective-permute-start.15 = (bf16[2,2,32,256]{3,2,1,0:T(8,128)(2,1)S(1)}, bf16[2,2,32,256]{3,2,1,0:T(8,128)(2,1)S(1)}, u32[]{:S(2)}, u32[]{:S(2)}) collective-permute-start(bf16[2,2,32,256]{3,2,1,0:T(8,128)(2,1)S(1)} %get-tuple-element.35), channel_id=1, source_target_pairs={{0,10},{1,11},{2,8},{3,9},{4,14},{5,15},{6,12},{7,13},{8,2},{9,3},... | collective-permute-start | bytes 196616 | tf_op jit(solution)/shard_map/ppermute | solution.py:578
  50.2 1.5 %collective-permute-start.16 = (bf16[2,2,32,256]{3,2,1,0:T(8,128)(2,1)S(1)}, bf16[2,2,32,256]{3,2,1,0:T(8,128)(2,1)S(1)}, u32[]{:S(2)}, u32[]{:S(2)}) collective-permute-start(bf16[2,2,32,256]{3,2,1,0:T(8,128)(2,1)S(1)} %get-tuple-element.36), channel_id=1, source_target_pairs={{0,12},{1,13},{2,14},{3,15},{4,8},{5,9},{6,10},{7,11},{8,4},{9,5},... | collective-permute-start | bytes 196616 | tf_op jit(solution)/shard_map/ppermute | solution.py:578
  51.7 2.3 %collective-permute-start.17 = (bf16[2,2,32,256]{3,2,1,0:T(8,128)(2,1)S(1)}, bf16[2,2,32,256]{3,2,1,0:T(8,128)(2,1)S(1)}, u32[]{:S(2)}, u32[]{:S(2)}) collective-permute-start(bf16[2,2,32,256]{3,2,1,0:T(8,128)(2,1)S(1)} %pad_maximum_fusion.15), channel_id=1, source_target_pairs={{0,14},{1,15},{2,12},{3,13},{4,10},{5,11},{6,8},{7,9},{8,6},{9,7},... | collective-permute-start | bytes 196616 | tf_op jit(solution)/shard_map/ppermute | solution.py:578
  54.0 2.1 %feed.2.refs_10_ = bf16[32,32,256]{2,1,0:T(8,128)(2,1)} custom-call(bf16[2,2,32,256]{3,2,1,0:T(8,128)(2,1)S(1)} %get-tuple-element.71.refs_0_, bf16[2,2,32,256]{3,2,1,0:T(8,128)(2,1)S(1)} %collective-permute-done.13.refs_1_, bf16[2,2,32,256]{3,2,1,0:T(8,128)(2,1)S(1)} %collective-permute-done.18.refs_2_, ...), custom_call_target="tpu_custom_call" | custom-call | flops 536870912 | bytes 2000000 | tf_op jit(solution)/shard_map/feed/pallas_call | solution.py:519
  56.2 3.2 %collective-permute-done.15.refs_1_ = bf16[2,2,32,256]{3,2,1,0:T(8,128)(2,1)S(1)} collective-permute-done((bf16[2,2,32,256]{3,2,1,0:T(8,128)(2,1)S(1)}, bf16[2,2,32,256]{3,2,1,0:T(8,128)(2,1)S(1)}, u32[]{:S(2)}, u32[]{:S(2)}) %collective-permute-start.15) | collective-permute-done | bytes 65568 | tf_op jit(solution)/shard_map/ppermute | solution.py:578
  59.3 2.1 %feed.3 = bf16[32,32,256]{2,1,0:T(8,128)(2,1)} custom-call(bf16[2,2,32,256]{3,2,1,0:T(8,128)(2,1)S(1)} %collective-permute-done.14.refs_0_, bf16[2,2,32,256]{3,2,1,0:T(8,128)(2,1)S(1)} %collective-permute-done.15.refs_1_, bf16[2,2,32,256]{3,2,1,0:T(8,128)(2,1)S(1)} %collective-permute-done.16.refs_2_, ...), custom_call_target="tpu_custom_call", output_to_operand_aliasing={{}: (10, {})} | custom-call | flops 536870912 | bytes 2000000 | tf_op jit(solution)/shard_map/feed/pallas_call | solution.py:519
  (88 shorter events, 7.1 us)
Async XLA Ops:
  1.1 1.4 %collective-permute-start = (bf16[32,256]{1,0:T(8,128)(2,1)S(1)}, bf16[32,256]{1,0:T(8,128)(2,1)S(1)}, u32[]{:S(2)}, u32[]{:S(2)}) collective-permute-start(bf16[32,256]{1,0:T(8,128)(2,1)S(1)} %border.1), channel_id=1, source_target_pairs={{0,1},{1,0},{2,3},{3,2},{4,5},{5,4},{6,7},{7,6},{8,9},{9,8},{10,11... | collective-permute-start | bytes 49160 | tf_op jit(solution)/shard_map/ppermute | solution.py:580
  2.7 5.6 %collective-permute-start.1 = (bf16[48,256]{1,0:T(8,128)(2,1)S(1)}, bf16[48,256]{1,0:T(8,128)(2,1)S(1)}, u32[]{:S(2)}, u32[]{:S(2)}) collective-permute-start(bf16[48,256]{1,0:T(8,128)(2,1)S(1)} %get-tuple-element.23), channel_id=1, source_target_pairs={{0,2},{2,0},{4,6},{6,4},{8,10},{10,8},{12,14},{14,12},{1,3},{3,1},... | collective-permute-start | bytes 73736 | tf_op jit(solution)/shard_map/ppermute | solution.py:586
  5.6 2.7 %collective-permute-start.2 = (bf16[48,256]{1,0:T(8,128)(2,1)S(1)}, bf16[48,256]{1,0:T(8,128)(2,1)S(1)}, u32[]{:S(2)}, u32[]{:S(2)}) collective-permute-start(bf16[48,256]{1,0:T(8,128)(2,1)S(1)} %get-tuple-element.24), channel_id=1, source_target_pairs={{2,4},{6,8},{10,12},{4,2},{8,6},{12,10},{3,5},{7,9},{11,13},{5,3},... | collective-permute-start | bytes 73736 | tf_op jit(solution)/shard_map/ppermute | solution.py:585
  11.8 24.0 %copy-start.11 = (bf16[256,768]{1,0:T(8,128)(2,1)S(1)}, bf16[256,768]{1,0:T(8,128)(2,1)}, u32[]{:S(2)}) copy-start(bf16[256,768]{1,0:T(8,128)(2,1)} %refs_10_.1) | copy-start | bytes 1179652
  11.8 24.0 %copy-start.12 = (bf16[256,256]{1,0:T(8,128)(2,1)S(1)}, bf16[256,256]{1,0:T(8,128)(2,1)}, u32[]{:S(2)}) copy-start(bf16[256,256]{1,0:T(8,128)(2,1)} %refs_11_.1) | copy-start | bytes 393220
  11.8 24.0 %copy-start.19 = (f32[256]{0:T(256)S(1)}, f32[256]{0:T(256)}, u32[]{:S(2)}) copy-start(f32[256]{0:T(256)} %param.29) | copy-start | bytes 3076
  11.8 24.0 %copy-start.20 = (f32[256]{0:T(256)S(1)}, f32[256]{0:T(256)}, u32[]{:S(2)}) copy-start(f32[256]{0:T(256)} %param.30) | copy-start | bytes 3076
  14.9 1.4 %collective-permute-start.7 = (bf16[2,2,2,32,256]{4,3,2,1,0:T(8,128)(2,1)S(1)}, bf16[2,2,2,32,256]{4,3,2,1,0:T(8,128)(2,1)S(1)}, u32[]{:S(2)}, u32[]{:S(2)}) collective-permute-start(bf16[2,2,2,32,256]{4,3,2,1,0:T(8,128)(2,1)S(1)} %get-tuple-element.31), channel_id=1, source_target_pairs={{0,1},{1,0},{2,3},{3,2},{4,5},{5,4},{6,7},{7,6},{8,9},{9,8},{10,11... | collective-permute-start | bytes 393224 | tf_op jit(solution)/shard_map/ppermute | solution.py:578
  14.9 13.0 %collective-permute-start.3 = (bf16[2,2,2,32,256]{4,3,2,1,0:T(8,128)(2,1)S(1)}, bf16[2,2,2,32,256]{4,3,2,1,0:T(8,128)(2,1)S(1)}, u32[]{:S(2)}, u32[]{:S(2)}) collective-permute-start(bf16[2,2,2,32,256]{4,3,2,1,0:T(8,128)(2,1)S(1)} %get-tuple-element.29), channel_id=1, source_target_pairs={{0,1},{1,0},{2,3},{3,2},{4,5},{5,4},{6,7},{7,6},{8,9},{9,8},{10,11... | collective-permute-start | bytes 393224 | tf_op jit(solution)/shard_map/ppermute | solution.py:578
  16.3 13.2 %collective-permute-start.11 = (bf16[2,2,32,256]{3,2,1,0:T(8,128)(2,1)S(1)}, bf16[2,2,32,256]{3,2,1,0:T(8,128)(2,1)S(1)}, u32[]{:S(2)}, u32[]{:S(2)}) collective-permute-start(bf16[2,2,32,256]{3,2,1,0:T(8,128)(2,1)S(1)} %pad_maximum_fusion.7), channel_id=1, source_target_pairs={{0,14},{1,15},{2,12},{3,13},{4,10},{5,11},{6,8},{7,9},{8,6},{9,7},... | collective-permute-start | bytes 196616 | tf_op jit(solution)/shard_map/ppermute | solution.py:578
  20.5 9.6 %collective-permute-start.10 = (bf16[2,2,32,256]{3,2,1,0:T(8,128)(2,1)S(1)}, bf16[2,2,32,256]{3,2,1,0:T(8,128)(2,1)S(1)}, u32[]{:S(2)}, u32[]{:S(2)}) collective-permute-start(bf16[2,2,32,256]{3,2,1,0:T(8,128)(2,1)S(1)} %pad_maximum_fusion.6), channel_id=1, source_target_pairs={{0,12},{1,13},{2,14},{3,15},{4,8},{5,9},{6,10},{7,11},{8,4},{9,5},... | collective-permute-start | bytes 196616 | tf_op jit(solution)/shard_map/ppermute | solution.py:578
  24.0 10.8 %collective-permute-start.9 = (bf16[2,2,32,256]{3,2,1,0:T(8,128)(2,1)S(1)}, bf16[2,2,32,256]{3,2,1,0:T(8,128)(2,1)S(1)}, u32[]{:S(2)}, u32[]{:S(2)}) collective-permute-start(bf16[2,2,32,256]{3,2,1,0:T(8,128)(2,1)S(1)} %pad_maximum_fusion.5), channel_id=1, source_target_pairs={{0,10},{1,11},{2,8},{3,9},{4,14},{5,15},{6,12},{7,13},{8,2},{9,3},... | collective-permute-start | bytes 196616 | tf_op jit(solution)/shard_map/ppermute | solution.py:578
  25.9 9.5 %collective-permute-start.8 = (bf16[2,2,32,256]{3,2,1,0:T(8,128)(2,1)S(1)}, bf16[2,2,32,256]{3,2,1,0:T(8,128)(2,1)S(1)}, u32[]{:S(2)}, u32[]{:S(2)}) collective-permute-start(bf16[2,2,32,256]{3,2,1,0:T(8,128)(2,1)S(1)} %pad_maximum_fusion.4), channel_id=1, source_target_pairs={{0,8},{1,9},{2,10},{3,11},{4,12},{5,13},{6,14},{7,15},{8,0},{9,1},... | collective-permute-start | bytes 196616 | tf_op jit(solution)/shard_map/ppermute | solution.py:578
  28.0 7.5 %collective-permute-start.6 = (bf16[2,2,32,256]{3,2,1,0:T(8,128)(2,1)S(1)}, bf16[2,2,32,256]{3,2,1,0:T(8,128)(2,1)S(1)}, u32[]{:S(2)}, u32[]{:S(2)}) collective-permute-start(bf16[2,2,32,256]{3,2,1,0:T(8,128)(2,1)S(1)} %pad_maximum_fusion.3), channel_id=1, source_target_pairs={{0,6},{1,7},{2,4},{3,5},{4,2},{5,3},{6,0},{7,1},{8,14},{9,15},{10,... | collective-permute-start | bytes 196616 | tf_op jit(solution)/shard_map/ppermute | solution.py:578
  29.5 6.3 %collective-permute-start.5 = (bf16[2,2,32,256]{3,2,1,0:T(8,128)(2,1)S(1)}, bf16[2,2,32,256]{3,2,1,0:T(8,128)(2,1)S(1)}, u32[]{:S(2)}, u32[]{:S(2)}) collective-permute-start(bf16[2,2,32,256]{3,2,1,0:T(8,128)(2,1)S(1)} %pad_maximum_fusion.2), channel_id=1, source_target_pairs={{0,4},{1,5},{2,6},{3,7},{4,0},{5,1},{6,2},{7,3},{8,12},{9,13},{10,... | collective-permute-start | bytes 196616 | tf_op jit(solution)/shard_map/ppermute | solution.py:578
  30.2 5.7 %collective-permute-start.4 = (bf16[2,2,32,256]{3,2,1,0:T(8,128)(2,1)S(1)}, bf16[2,2,32,256]{3,2,1,0:T(8,128)(2,1)S(1)}, u32[]{:S(2)}, u32[]{:S(2)}) collective-permute-start(bf16[2,2,32,256]{3,2,1,0:T(8,128)(2,1)S(1)} %pad_maximum_fusion.1), channel_id=1, source_target_pairs={{0,2},{1,3},{2,0},{3,1},{4,6},{5,7},{6,4},{7,5},{8,10},{9,11},{10,... | collective-permute-start | bytes 196616 | tf_op jit(solution)/shard_map/ppermute | solution.py:578
  38.6 1.6 %collective-permute-start.12 = (bf16[4,2,2,32,256]{4,3,2,1,0:T(8,128)(2,1)S(1)}, bf16[4,2,2,32,256]{4,3,2,1,0:T(8,128)(2,1)S(1)}, u32[]{:S(2)}, u32[]{:S(2)}) collective-permute-start(bf16[4,2,2,32,256]{4,3,2,1,0:T(8,128)(2,1)S(1)} %get-tuple-element.33), channel_id=1, source_target_pairs={{0,1},{1,0},{2,3},{3,2},{4,5},{5,4},{6,7},{7,6},{8,9},{9,8},{10,11... | collective-permute-start | bytes 786440 | tf_op jit(solution)/shard_map/ppermute | solution.py:578
  40.3 4.3 %collective-permute-start.13 = (bf16[2,2,32,256]{3,2,1,0:T(8,128)(2,1)S(1)}, bf16[2,2,32,256]{3,2,1,0:T(8,128)(2,1)S(1)}, u32[]{:S(2)}, u32[]{:S(2)}) collective-permute-start(bf16[2,2,32,256]{3,2,1,0:T(8,128)(2,1)S(1)} %pad_maximum_fusion.8), channel_id=1, source_target_pairs={{0,2},{1,3},{2,0},{3,1},{4,6},{5,7},{6,4},{7,5},{8,10},{9,11},{10,... | collective-permute-start | bytes 196616 | tf_op jit(solution)/shard_map/ppermute | solution.py:578
  41.2 10.5 %collective-permute-start.19 = (bf16[2,2,32,256]{3,2,1,0:T(8,128)(2,1)S(1)}, bf16[2,2,32,256]{3,2,1,0:T(8,128)(2,1)S(1)}, u32[]{:S(2)}, u32[]{:S(2)}) collective-permute-start(bf16[2,2,32,256]{3,2,1,0:T(8,128)(2,1)S(1)} %pad_maximum_fusion.11), channel_id=1, source_target_pairs={{0,6},{1,7},{2,4},{3,5},{4,2},{5,3},{6,0},{7,1},{8,14},{9,15},{10,... | collective-permute-start | bytes 196616 | tf_op jit(solution)/shard_map/ppermute | solution.py:578
  42.7 11.3 %collective-permute-start.18 = (bf16[2,2,32,256]{3,2,1,0:T(8,128)(2,1)S(1)}, bf16[2,2,32,256]{3,2,1,0:T(8,128)(2,1)S(1)}, u32[]{:S(2)}, u32[]{:S(2)}) collective-permute-start(bf16[2,2,32,256]{3,2,1,0:T(8,128)(2,1)S(1)} %pad_maximum_fusion.10), channel_id=1, source_target_pairs={{0,4},{1,5},{2,6},{3,7},{4,0},{5,1},{6,2},{7,3},{8,12},{9,13},{10,... | collective-permute-start | bytes 196616 | tf_op jit(solution)/shard_map/ppermute | solution.py:578
  44.6 11.6 %collective-permute-start.14 = (bf16[2,2,32,256]{3,2,1,0:T(8,128)(2,1)S(1)}, bf16[2,2,32,256]{3,2,1,0:T(8,128)(2,1)S(1)}, u32[]{:S(2)}, u32[]{:S(2)}) collective-permute-start(bf16[2,2,32,256]{3,2,1,0:T(8,128)(2,1)S(1)} %get-tuple-element.34), channel_id=1, source_target_pairs={{0,8},{1,9},{2,10},{3,11},{4,12},{5,13},{6,14},{7,15},{8,0},{9,1},... | collective-permute-start | bytes 196616 | tf_op jit(solution)/shard_map/ppermute | solution.py:578
  48.3 11.1 %collective-permute-start.15 = (bf16[2,2,32,256]{3,2,1,0:T(8,128)(2,1)S(1)}, bf16[2,2,32,256]{3,2,1,0:T(8,128)(2,1)S(1)}, u32[]{:S(2)}, u32[]{:S(2)}) collective-permute-start(bf16[2,2,32,256]{3,2,1,0:T(8,128)(2,1)S(1)} %get-tuple-element.35), channel_id=1, source_target_pairs={{0,10},{1,11},{2,8},{3,9},{4,14},{5,15},{6,12},{7,13},{8,2},{9,3},... | collective-permute-start | bytes 196616 | tf_op jit(solution)/shard_map/ppermute | solution.py:578
  50.2 9.2 %collective-permute-start.16 = (bf16[2,2,32,256]{3,2,1,0:T(8,128)(2,1)S(1)}, bf16[2,2,32,256]{3,2,1,0:T(8,128)(2,1)S(1)}, u32[]{:S(2)}, u32[]{:S(2)}) collective-permute-start(bf16[2,2,32,256]{3,2,1,0:T(8,128)(2,1)S(1)} %get-tuple-element.36), channel_id=1, source_target_pairs={{0,12},{1,13},{2,14},{3,15},{4,8},{5,9},{6,10},{7,11},{8,4},{9,5},... | collective-permute-start | bytes 196616 | tf_op jit(solution)/shard_map/ppermute | solution.py:578
  51.7 7.7 %collective-permute-start.17 = (bf16[2,2,32,256]{3,2,1,0:T(8,128)(2,1)S(1)}, bf16[2,2,32,256]{3,2,1,0:T(8,128)(2,1)S(1)}, u32[]{:S(2)}, u32[]{:S(2)}) collective-permute-start(bf16[2,2,32,256]{3,2,1,0:T(8,128)(2,1)S(1)} %pad_maximum_fusion.15), channel_id=1, source_target_pairs={{0,14},{1,15},{2,12},{3,13},{4,10},{5,11},{6,8},{7,9},{8,6},{9,7},... | collective-permute-start | bytes 196616 | tf_op jit(solution)/shard_map/ppermute | solution.py:578
  (17 other events, 173.9 us)

commit v2 on v1

--- a/solution.py
+++ b/solution.py
@@ -253,19 +253,9 @@
     )(even, odd, outer, w_expand, vectors)
 
 
-def conv_kernel(
-    far,
-    expanded_ref,
-    image_ref,
-    tap_ref,
-    outer_ref,
-    w_project_ref,
-    vectors_ref,
-    own_ref,
-    core_ref,
-    section_ref,
-    deep_ref,
-):
+def conv_kernel(expanded_ref, image_ref, tap_ref, outer_ref, w_project_ref, vectors_ref, *refs):
+    out_refs = (refs[2:4], refs[:2])
+    section_ref, deep_ref = refs[4:]
     place = Place()
     rows, cols, width = image_ref.shape
     hidden = expanded_ref.shape[-1]
@@ -273,8 +263,6 @@
     octets = cols // SLAB
     half = SLAB // 2
     zi, xc = place.zi, place.xc
-    pair = jnp.bitwise_xor(zi // 2, far) * 2
-    at_top = pair == 0
     ok_up, ok_down = place.strip > 0, place.strip < place.strips - 1
     slab_id = lax.broadcasted_iota(jnp.int32, (SLAB, LANES), 0)
 
@@ -282,73 +270,64 @@
         lanes = pl.ds(pl.multiple_of(index * LANES, LANES), LANES)
         weights = [vectors_ref[ROW_TAPS + t : ROW_TAPS + t + 1, lanes] for t in range(9)]
         bias = vectors_ref[ROW_DEPTH : ROW_DEPTH + 1, lanes]
-        outer = outer_ref[:, lanes].astype(F32)
-        above_all = jnp.where(ok_up, outer, 0.0)
-        below_all = jnp.where(ok_down, outer, 0.0)
         for m in range(groups):
             for p in range(2):
-                start = m * SLAB + p * half + pair
+                start = m * SLAB + p * half
                 lines = []
-                for q in range(4):
-                    r = start + q - 1
-                    if m == 0 and p == 0 and q == 0:
-                        inside = expanded_ref[jnp.maximum(r, 0), :, lanes].astype(F32)
-                        lines.append(jnp.where(at_top, above_all, inside))
-                    elif m == groups - 1 and p == 1 and q == 3:
-                        inside = expanded_ref[jnp.minimum(r, rows - 1), :, lanes].astype(F32)
-                        lines.append(jnp.where(at_top, inside, below_all))
+                for r in range(start - 1, start + half + 1):
+                    if r < 0:
+                        lines.append(jnp.where(ok_up, outer_ref[:, lanes].astype(F32), 0.0))
+                    elif r >= rows:
+                        lines.append(jnp.where(ok_down, outer_ref[:, lanes].astype(F32), 0.0))
                     else:
                         lines.append(expanded_ref[r, :, lanes].astype(F32))
-                for i in range(2):
+                for q in range(half):
+                    r = start + q
                     sums = [
-                        lines[i] * weights[j] + lines[i + 1] * weights[3 + j] + lines[i + 2] * weights[6 + j]
+                        lines[q] * weights[j] + lines[q + 1] * weights[3 + j] + lines[q + 2] * weights[6 + j]
                         for j in range(3)
                     ]
-                    within = p * half + pair + i
-                    left = pltpu.roll(tap_ref[0, m * SLAB : (m + 1) * SLAB, lanes], (SLAB - within) % SLAB, 0)
-                    right = pltpu.roll(tap_ref[1, m * SLAB : (m + 1) * SLAB, lanes], SLAB - 1 - within, 0)
                     before, after = pltpu.roll(sums[0], 1, 0), pltpu.roll(sums[2], cols - 1, 0)
-                    head = jnp.where(slab_id == 0, left, before[:SLAB])
-                    tail = jnp.where(slab_id == SLAB - 1, right, after[-SLAB:])
+                    head = jnp.where(slab_id == 0, tap_ref[0, r : r + 1, lanes], before[:SLAB])
+                    tail = jnp.where(slab_id == SLAB - 1, tap_ref[1, r : r + 1, lanes], after[-SLAB:])
                     before = jnp.concatenate([head, before[SLAB:]], axis=0)
                     after = jnp.concatenate([after[:-SLAB], tail], axis=0)
-                    deep_ref[p, i, m, :, lanes] = gelu(before + sums[1] + after + bias).astype(BF16)
+                    deep_ref[p, q, m, :, lanes] = gelu(before + sums[1] + after + bias).astype(BF16)
         return carry
 
     lax.fori_loop(0, hidden // LANES, chunk, 0)
 
     b_project = vectors_ref[ROW_PROJECT : ROW_PROJECT + 1, :width]
-    for k in range(2):
-        i = jnp.bitwise_xor(zi % 2, k)
+    for k in range(4):
+        q = jnp.bitwise_xor(zi, k)
         for p in range(2):
-            projected = dot(deep_ref[p, i].reshape(groups * cols, hidden), w_project_ref[...]) + b_project
-            own = jnp.stack([image_ref[m * SLAB + p * half + pair + i] for m in range(groups)]).astype(F32)
+            projected = dot(deep_ref[p, q].reshape(groups * cols, hidden), w_project_ref[...]) + b_project
+            own = jnp.stack([image_ref[m * SLAB + p * half + q] for m in range(groups)]).astype(F32)
             section = (own + projected.reshape(groups, cols, width)).reshape(groups, octets, SLAB, width)
             for o in range(octets):
                 section_ref[k, p, o] = section[:, o].reshape(groups * SLAB, width)
             for j in range(4):
-                ref = core_ref if j % 2 else own_ref
-                ref[k, j // 2, p] = section_ref[k, p, jnp.bitwise_xor(xc, j)].astype(BF16)
-
-
-def conv(far, expanded, image, taps, outer, w_project, vectors):
+                out_refs[k // 2][j % 2][k % 2, j // 2, p] = section_ref[k, p, jnp.bitwise_xor(xc, j)].astype(BF16)
+
+
+def conv(expanded, image, taps, outer, w_project, vectors):
     rows, cols, width = image.shape
     hidden = expanded.shape[-1]
     groups = rows // SLAB
     octets = cols // SLAB
     shape = jax.ShapeDtypeStruct((2, 2, 2, groups * SLAB, width), BF16)
     return pl.pallas_call(
-        functools.partial(conv_kernel, far),
+        conv_kernel,
         in_specs=[VMEM] * 6,
-        out_specs=[VMEM] * 2,
-        out_shape=[shape] * 2,
+        out_specs=[VMEM] * 4,
+        out_shape=[shape] * 4,
         scratch_shapes=[
-            pltpu.VMEM((2, 2, octets, groups * SLAB, width), F32),
-            pltpu.VMEM((2, 2, groups, cols, hidden), BF16),
+            pltpu.VMEM((4, 2, octets, groups * SLAB, width), F32),
+            pltpu.VMEM((2, 4, groups, cols, hidden), BF16),
         ],
         compiler_params=PARAMS,
         cost_estimate=pl.CostEstimate(
-            flops=rows * cols * width * hidden, bytes_accessed=6_000_000, transcendentals=rows * cols * hidden
+            flops=2 * rows * cols * width * hidden, bytes_accessed=6_000_000, transcendentals=rows * cols * hidden
         ),
         name="conv",
     )(expanded, image, taps, outer, w_project, vectors)
@@ -356,8 +335,9 @@
 
 def attend_kernel(heads, *refs):
     in_refs, refs = refs[:8], refs[8:]
-    gain_ref, shift_ref, w_qkv_ref, w_out_ref, table_ref, own_ref, core_ref = refs[:7]
-    token_ref, normed_ref, query_t_ref, value_t_ref, bias_ref, window_ref, key_ref, qt_ref, vt_ref, context_ref = refs[7:]
+    gain_ref, shift_ref, w_qkv_ref, w_out_ref, table_ref = refs[:5]
+    out_refs = (refs[7:9], refs[5:7])
+    token_ref, normed_ref, query_t_ref, value_t_ref, bias_ref, window_ref, key_ref, qt_ref, vt_ref, context_ref = refs[9:]
     place = Place()
     zi, xc = place.zi, place.xc
     halves, count, _ = normed_ref.shape
@@ -435,10 +415,10 @@
     for k in range(4):
         for j in range(4):
             slot = slot_of(k, j)
-            ref = core_ref if j % 2 else own_ref
+            ref = out_refs[k // 2][j % 2]
             for p in range(2):
                 added = jnp.concatenate([normed_ref[c, spot_of(p, slot), :] for c in range(halves)], axis=1)
-                ref[k, j // 2, p] = (token_ref[p, slot] + added).astype(BF16)
+                ref[k % 2, j // 2, p] = (token_ref[p, slot] + added).astype(BF16)
 
 
 def attend(arrived, heads, weights):
@@ -446,12 +426,12 @@
     count = 32 * chunk_rows
     flops = 2 * count * width * (4 * width)
     tokens = GRID * GRID
-    shape = jax.ShapeDtypeStruct((4, 2, 2, chunk_rows, width), BF16)
+    shape = jax.ShapeDtypeStruct((2, 2, 2, chunk_rows, width), BF16)
     return pl.pallas_call(
         functools.partial(attend_kernel, heads),
         in_specs=[VMEM] * 13,
-        out_specs=[VMEM] * 2,
-        out_shape=[shape] * 2,
+        out_specs=[VMEM] * 4,
+        out_shape=[shape] * 4,
         scratch_shapes=[
             pltpu.VMEM((2, 16, chunk_rows, width), F32),
             pltpu.VMEM((width // LANES, count, LANES), F32),
@@ -470,63 +450,60 @@
     )(*arrived, *weights)
 
 
-def feed_kernel(far, *refs):
-    in_refs, refs = refs[:4], refs[4:]
+def feed_kernel(places, *refs):
+    parts = 2 * len(places)
+    in_refs, refs = refs[:parts], refs[parts:]
     gain_ref, shift_ref, w_up_ref, b_up_ref, w_down_ref, b_down_ref = refs[:6]
     out_ref, line_ref, section_ref, sems = refs[-4:]
     place = Place()
     zi, xc = place.zi, place.xc
-    groups, _, _, cols, width = line_ref.shape
+    _, _, groups, cols, width = line_ref.shape
     half = SLAB // 2
-    pair = jnp.bitwise_xor(zi // 2, far) * 2
     step = 2 * LANES
-    for k in range(2):
-        i = jnp.bitwise_xor(zi % 2, k)
+    copies = []
+    for n, k in enumerate(places):
         for p in range(2):
             for j in range(4):
                 o = jnp.bitwise_xor(xc, j)
-                section_ref[k, p, o] = in_refs[2 * k + j // 2][j % 2, p].astype(F32)
-            slabs = [section_ref[k, p, o].reshape(groups, 1, SLAB, width) for o in range(cols // SLAB)]
+                section_ref[n, p, o] = in_refs[2 * n + j // 2][j % 2, p].astype(F32)
+            slabs = [section_ref[n, p, o].reshape(groups, 1, SLAB, width) for o in range(cols // SLAB)]
             section = jnp.concatenate(slabs, axis=1).reshape(groups * cols, width)
             normed = layer_norm(section, gain_ref[...], shift_ref[...]).astype(BF16)
             total = section + b_down_ref[...]
-            for n in range(w_up_ref.shape[1] // step):
-                inner = slice(n * step, (n + 1) * step)
+            for i in range(w_up_ref.shape[1] // step):
+                inner = slice(i * step, (i + 1) * step)
                 hidden = gelu(dot(normed, w_up_ref[:, inner]) + b_up_ref[:, inner]).astype(BF16)
                 total = total + dot(hidden, w_down_ref[inner, :])
-            result = total.reshape(groups, cols, width).astype(BF16)
+            line_ref[n, p] = total.reshape(groups, cols, width).astype(BF16)
             for m in range(groups):
-                line_ref[m, p, i] = result[m]
-    copies = [
-        pltpu.make_async_copy(
-            line_ref.at[m, p], out_ref.at[pl.ds(m * SLAB + p * half + pair, 2)], sems.at[2 * m + p]
-        )
-        for m in range(groups)
-        for p in range(2)
-    ]
+                r = m * SLAB + p * half + jnp.bitwise_xor(zi, k)
+                copies.append(
+                    pltpu.make_async_copy(line_ref.at[n, p, m], out_ref.at[r], sems.at[len(copies)])
+                )
     for copy in copies:
         copy.start()
     for copy in copies:
         copy.wait()
 
 
-def feed(far, sections, weights, image, partial):
+def feed(places, sections, weights, image, partial):
     rows, cols, width = image.shape
     groups = rows // SLAB
     hidden = weights[2].shape[1]
-    count = rows * cols // 2
+    held = len(sections) + len(weights)
+    count = len(places) * rows * cols // 4
     extra = [] if partial is None else [partial]
     return pl.pallas_call(
-        functools.partial(feed_kernel, far),
-        in_specs=[VMEM] * 10 + [ANY] * len(extra),
+        functools.partial(feed_kernel, places),
+        in_specs=[VMEM] * held + [ANY] * len(extra),
         out_specs=ANY,
         out_shape=jax.ShapeDtypeStruct(image.shape, BF16),
         scratch_shapes=[
-            pltpu.VMEM((groups, 2, 2, cols, width), BF16),
-            pltpu.VMEM((2, 2, cols // SLAB, groups * SLAB, width), F32),
-            pltpu.SemaphoreType.DMA((2 * groups,)),
+            pltpu.VMEM((len(places), 2, groups, cols, width), BF16),
+            pltpu.VMEM((len(places), 2, cols // SLAB, groups * SLAB, width), F32),
+            pltpu.SemaphoreType.DMA((2 * len(places) * groups,)),
         ],
-        input_output_aliases={10: 0} if extra else {},
+        input_output_aliases={held: 0} if extra else {},
         compiler_params=PARAMS,
         cost_estimate=pl.CostEstimate(
             flops=4 * count * width * hidden, bytes_accessed=2_000_000, transcendentals=count * hidden
@@ -606,23 +583,17 @@
             (first + k, x): jnp.stack([own[k, x], from_core[k, x]]) for k in range(own.shape[0]) for x in range(2)
         }
 
-    own, to_core = conv(0, expanded, image, taps, outer, w_project, vectors)
-    outgoing = paired(own, exchange(to_core, 1), 0)
-    arrived = {(0, 0): outgoing[0, 0]}
-    arrived.update({key: to_peer(outgoing, key) for key in near_keys})
-    own, to_core = conv(1, expanded, image, taps, outer, w_project, vectors)
-    outgoing = paired(own, exchange(to_core, 1), 2)
-    arrived.update({key: to_peer(outgoing, key) for key in far_keys})
-    order = [(k, x) for k in range(4) for x in range(2)]
-    own, to_core = attend([arrived[key] for key in order], heads, attend_weights)
-
-    outgoing = paired(own, exchange(to_core, 1), 0)
-    home = {(0, 0): outgoing[0, 0]}
-    home.update({key: to_peer(outgoing, key) for key in near_keys})
-    home[0, 1], outgoing = after(home[0, 1], outgoing)
-    home.update({key: to_peer(outgoing, key) for key in far_keys})
-    out = feed(0, [home[key] for key in order[:4]], feed_weights, image, None)
-    return feed(1, [home[key] for key in order[4:]], feed_weights, image, out)
+    def spread(own_f, to_core_f, own_n, to_core_n):
+        outgoing = paired(own_f, exchange(to_core_f, 1), 2)
+        arrived = {key: to_peer(outgoing, key) for key in far_keys}
+        outgoing = paired(own_n, exchange(to_core_n, 1), 0)
+        arrived[0, 0] = outgoing[0, 0]
+        arrived.update({key: to_peer(outgoing, key) for key in near_keys})
+        return [arrived[k, x] for k in range(4) for x in range(2)]
+
+    held = spread(*conv(expanded, image, taps, outer, w_project, vectors))
+    home = spread(*attend(held, heads, attend_weights))
+    return feed((0, 1, 2, 3), home, feed_weights, image, None)
 
 
 def solution(mesh):

time: 61.6 us -> 60.2 us (0.977)
  Pallas kernels: 15.6 us -> 14.2 us
    pallas_call x4 -> x2, Pallas kernels: 10.3 us -> 8.87 us  [the longest x1 5.35 us: conv(): pl.pallas_call(conv_kernel, in_specs=[VMEM] * 6, out_specs=[VMEM] * 4, ou...]
    ppermute x17 -> x18, waiting for transfers between devices: 9.42 us -> 9.25 us  [exchange(): return lax.ppermute(value, ('tile', 'strip'), pairs)]
    ppermute x17 -> x18, starting transfers between devices: 29.7 us -> 29.8 us  [exchange(): return lax.ppermute(value, ('tile', 'strip'), pairs)]
  transfers between devices with their start and end apart: 20 -> 21, of which waited for: 8 -> 10; matrix products, arithmetic and copies ran while one was open for 0% -> 0% of each run, Pallas kernels for 7% -> 3%
where the time goes in v2:
time: 60.2 us; the launch traced here: 60.1 us
  starting transfers between devices  33.9 us (56%)
  Pallas kernels  14.2 us (24%)
  waiting for transfers between devices  10.1 us (17%)
  local copies, waits for them, and re-layouts  1.23 us (2%)
    ppermute x18, starting transfers between devices, exchange(): return lax.ppermute(value, ('tile', 'strip'), pairs)  29.8 us
    ppermute x18, waiting for transfers between devices, exchange(): return lax.ppermute(value, ('tile', 'strip'), pairs)  9.25 us
    pallas_call x1, Pallas kernels, conv(): pl.pallas_call(conv_kernel, in_specs=[VMEM] * 6, out_specs=[VMEM] * 4, ou...  5.35 us
    pallas_call x1, Pallas kernels, feed(): pl.pallas_call(functools.partial(feed_kernel, places), in_specs=[VMEM] *...  3.52 us
    ppermute x1, starting transfers between devices, local(): even = lax.ppermute(to_even, 'tile', even_pairs)  2.9 us
    pallas_call x1, Pallas kernels, attend(): pl.pallas_call(functools.partial(attend_kernel, heads), in_specs=[VMEM] *...  2.78 us
    pallas_call x1, Pallas kernels, expand(): pl.pallas_call(expand_kernel, in_specs=[VMEM] * (2 + len(vectors)), out_s...  1.61 us
  transfers between devices with their start and end apart: 21, of which 10 were waited for; matrix products, arithmetic and copies ran while one was open for 0% of the time, Pallas kernels for 3%

profile of v2, /device:TPU:0, one launch (start us, length us, event | category | flops | bytes accessed | tf_op | source)
XLA Modules:
  0.0 60.1 jit_solution(12719433147788488367)
XLA Ops:
  0.0 1.0 %copy-done = bf16[32,32,256]{2,1,0:T(8,128)(2,1)S(1)} copy-done((bf16[32,32,256]{2,1,0:T(8,128)(2,1)S(1)}, bf16[32,32,256]{2,1,0:T(8,128)(2,1)}, u32[]{:S(2)}) %copy-start) | copy-done | bytes 524312
  1.6 0.8 %collective-permute-done.beyond_ref.outer_ref = bf16[32,256]{1,0:T(8,128)(2,1)S(1)} collective-permute-done((bf16[32,256]{1,0:T(8,128)(2,1)S(1)}, bf16[32,256]{1,0:T(8,128)(2,1)S(1)}, u32[]{:S(2)}, u32[]{:S(2)}) %collective-permute-start) | collective-permute-done | bytes 16416 | tf_op jit(solution)/shard_map/ppermute | solution.py:557
  2.7 2.9 %collective-permute-start.1 = (bf16[48,256]{1,0:T(8,128)(2,1)S(1)}, bf16[48,256]{1,0:T(8,128)(2,1)S(1)}, u32[]{:S(2)}, u32[]{:S(2)}) collective-permute-start(bf16[48,256]{1,0:T(8,128)(2,1)S(1)} %get-tuple-element.20), channel_id=1, source_target_pairs={{0,2},{2,0},{4,6},{6,4},{8,10},{10,8},{12,14},{14,12},{1,3},{3,1},... | collective-permute-start | bytes 73736 | tf_op jit(solution)/shard_map/ppermute | solution.py:563
  6.3 1.6 %expand.1 = (bf16[32,32,1024]{2,1,0:T(8,128)(2,1)S(1)}, f32[24,1024]{1,0:T(8,128)S(1)}) custom-call(bf16[32,32,256]{2,1,0:T(8,128)(2,1)S(1)} %copy-done, bf16[256,1024]{1,0:T(8,128)(2,1)S(1)} %copy-done.3, f32[1,256]{1,0:T(1,128)S(1)} %bitcast.78, f32[1,256]{1,0:T(1,128)S(1)} %bitcast.79, f32[1,1024]{1,0:T(1,128)S(1)} %bitcast.75, f32[1,1024]{1,0:T(1,128)S(1)} %bitcast.76, ...), custom_call_target="tpu_custom_call" | custom-call | flops 4294967296 | bytes 4000000 | tf_op jit(solution)/shard_map/expand/pallas_call | solution.py:176
  8.8 5.3 %conv.1 = (bf16[2,2,2,32,256]{4,3,2,1,0:T(8,128)(2,1)S(1)}, bf16[2,2,2,32,256]{4,3,2,1,0:T(8,128)(2,1)S(1)}, bf16[2,2,2,32,256]{4,3,2,1,0:T(8,128)(2,1)S(1)}, bf16[2,2,2,32,256]{4,3,2,1,0:T(8,128)(2,1)S(1)}) custom-call(bf16[32,32,1024]{2,1,0:T(8,128)(2,1)S(1)} %get-tuple-element.19.expanded_ref, bf16[32,32,256]{2,1,0:T(8,128)(2,1)S(1)} %copy-done.1, ...), custom_call_target="tpu_custom_call" | custom-call | flops 536870912 | bytes 6000000 | tf_op jit(solution)/shard_map/conv/pallas_call | solution.py:319
  14.8 0.8 %collective-permute-done.7 = bf16[2,2,2,32,256]{4,3,2,1,0:T(8,128)(2,1)S(1)} collective-permute-done((bf16[2,2,2,32,256]{4,3,2,1,0:T(8,128)(2,1)S(1)}, bf16[2,2,2,32,256]{4,3,2,1,0:T(8,128)(2,1)S(1)}, u32[]{:S(2)}, u32[]{:S(2)}) %collective-permute-start.7) | collective-permute-done | bytes 131104 | tf_op jit(solution)/shard_map/ppermute | solution.py:555
  15.6 4.2 %collective-permute-start.11 = (bf16[2,2,32,256]{3,2,1,0:T(8,128)(2,1)S(1)}, bf16[2,2,32,256]{3,2,1,0:T(8,128)(2,1)S(1)}, u32[]{:S(2)}, u32[]{:S(2)}) collective-permute-start(bf16[2,2,32,256]{3,2,1,0:T(8,128)(2,1)S(1)} %pad_maximum_fusion.7), channel_id=1, source_target_pairs={{0,14},{1,15},{2,12},{3,13},{4,10},{5,11},{6,8},{7,9},{8,6},{9,7},... | collective-permute-start | bytes 196616 | tf_op jit(solution)/shard_map/ppermute | solution.py:555
  19.9 3.4 %collective-permute-start.10 = (bf16[2,2,32,256]{3,2,1,0:T(8,128)(2,1)S(1)}, bf16[2,2,32,256]{3,2,1,0:T(8,128)(2,1)S(1)}, u32[]{:S(2)}, u32[]{:S(2)}) collective-permute-start(bf16[2,2,32,256]{3,2,1,0:T(8,128)(2,1)S(1)} %pad_maximum_fusion.6), channel_id=1, source_target_pairs={{0,12},{1,13},{2,14},{3,15},{4,8},{5,9},{6,10},{7,11},{8,4},{9,5},... | collective-permute-start | bytes 196616 | tf_op jit(solution)/shard_map/ppermute | solution.py:555
  23.3 1.9 %collective-permute-start.9 = (bf16[2,2,32,256]{3,2,1,0:T(8,128)(2,1)S(1)}, bf16[2,2,32,256]{3,2,1,0:T(8,128)(2,1)S(1)}, u32[]{:S(2)}, u32[]{:S(2)}) collective-permute-start(bf16[2,2,32,256]{3,2,1,0:T(8,128)(2,1)S(1)} %pad_maximum_fusion.5), channel_id=1, source_target_pairs={{0,10},{1,11},{2,8},{3,9},{4,14},{5,15},{6,12},{7,13},{8,2},{9,3},... | collective-permute-start | bytes 196616 | tf_op jit(solution)/shard_map/ppermute | solution.py:555
  25.3 2.0 %collective-permute-start.8 = (bf16[2,2,32,256]{3,2,1,0:T(8,128)(2,1)S(1)}, bf16[2,2,32,256]{3,2,1,0:T(8,128)(2,1)S(1)}, u32[]{:S(2)}, u32[]{:S(2)}) collective-permute-start(bf16[2,2,32,256]{3,2,1,0:T(8,128)(2,1)S(1)} %pad_maximum_fusion.4), channel_id=1, source_target_pairs={{0,8},{1,9},{2,10},{3,11},{4,12},{5,13},{6,14},{7,15},{8,0},{9,1},... | collective-permute-start | bytes 196616 | tf_op jit(solution)/shard_map/ppermute | solution.py:555
  27.3 1.5 %collective-permute-start.6 = (bf16[2,2,32,256]{3,2,1,0:T(8,128)(2,1)S(1)}, bf16[2,2,32,256]{3,2,1,0:T(8,128)(2,1)S(1)}, u32[]{:S(2)}, u32[]{:S(2)}) collective-permute-start(bf16[2,2,32,256]{3,2,1,0:T(8,128)(2,1)S(1)} %pad_maximum_fusion.3), channel_id=1, source_target_pairs={{0,6},{1,7},{2,4},{3,5},{4,2},{5,3},{6,0},{7,1},{8,14},{9,15},{10,... | collective-permute-start | bytes 196616 | tf_op jit(solution)/shard_map/ppermute | solution.py:555
  29.5 2.1 %collective-permute-start.4 = (bf16[2,2,32,256]{3,2,1,0:T(8,128)(2,1)S(1)}, bf16[2,2,32,256]{3,2,1,0:T(8,128)(2,1)S(1)}, u32[]{:S(2)}, u32[]{:S(2)}) collective-permute-start(bf16[2,2,32,256]{3,2,1,0:T(8,128)(2,1)S(1)} %pad_maximum_fusion.1), channel_id=1, source_target_pairs={{0,2},{1,3},{2,0},{3,1},{4,6},{5,7},{6,4},{7,5},{8,10},{9,11},{10,... | collective-permute-start | bytes 196616 | tf_op jit(solution)/shard_map/ppermute | solution.py:555
  31.7 2.3 %collective-permute-done.9.refs_5_ = bf16[2,2,32,256]{3,2,1,0:T(8,128)(2,1)S(1)} collective-permute-done((bf16[2,2,32,256]{3,2,1,0:T(8,128)(2,1)S(1)}, bf16[2,2,32,256]{3,2,1,0:T(8,128)(2,1)S(1)}, u32[]{:S(2)}, u32[]{:S(2)}) %collective-permute-start.9) | collective-permute-done | bytes 65568 | tf_op jit(solution)/shard_map/ppermute | solution.py:555
  34.1 0.7 %collective-permute-done.8.refs_4_ = bf16[2,2,32,256]{3,2,1,0:T(8,128)(2,1)S(1)} collective-permute-done((bf16[2,2,32,256]{3,2,1,0:T(8,128)(2,1)S(1)}, bf16[2,2,32,256]{3,2,1,0:T(8,128)(2,1)S(1)}, u32[]{:S(2)}, u32[]{:S(2)}) %collective-permute-start.8) | collective-permute-done | bytes 65568 | tf_op jit(solution)/shard_map/ppermute | solution.py:555
  35.2 2.8 %attend.1 = (bf16[2,2,2,32,256]{4,3,2,1,0:T(8,128)(2,1)S(1)}, bf16[2,2,2,32,256]{4,3,2,1,0:T(8,128)(2,1)S(1)}, bf16[2,2,2,32,256]{4,3,2,1,0:T(8,128)(2,1)S(1)}, bf16[2,2,2,32,256]{4,3,2,1,0:T(8,128)(2,1)S(1)}) custom-call(bf16[2,2,32,256]{3,2,1,0:T(8,128)(2,1)S(1)} %pad_maximum_fusion.refs_0_, bf16[2,2,32,256]{3,2,1,0:T(8,128)(2,1)S(1)} %collective-permute-done.4.refs_1_, ...), custom_call_target="tpu_custom_call" | custom-call | flops 536870912 | bytes 4000000 | tf_op jit(solution)/shard_map/attend/pallas_call | solution.py:430
  38.6 0.7 %collective-permute-done.16 = bf16[2,2,2,32,256]{4,3,2,1,0:T(8,128)(2,1)S(1)} collective-permute-done((bf16[2,2,2,32,256]{4,3,2,1,0:T(8,128)(2,1)S(1)}, bf16[2,2,2,32,256]{4,3,2,1,0:T(8,128)(2,1)S(1)}, u32[]{:S(2)}, u32[]{:S(2)}) %collective-permute-start.16) | collective-permute-done | bytes 131104 | tf_op jit(solution)/shard_map/ppermute | solution.py:555
  39.4 4.2 %collective-permute-start.20 = (bf16[2,2,32,256]{3,2,1,0:T(8,128)(2,1)S(1)}, bf16[2,2,32,256]{3,2,1,0:T(8,128)(2,1)S(1)}, u32[]{:S(2)}, u32[]{:S(2)}) collective-permute-start(bf16[2,2,32,256]{3,2,1,0:T(8,128)(2,1)S(1)} %pad_maximum_fusion.15), channel_id=1, source_target_pairs={{0,14},{1,15},{2,12},{3,13},{4,10},{5,11},{6,8},{7,9},{8,6},{9,7},... | collective-permute-start | bytes 196616 | tf_op jit(solution)/shard_map/ppermute | solution.py:555
  43.7 1.5 %collective-permute-start.18 = (bf16[2,2,32,256]{3,2,1,0:T(8,128)(2,1)S(1)}, bf16[2,2,32,256]{3,2,1,0:T(8,128)(2,1)S(1)}, u32[]{:S(2)}, u32[]{:S(2)}) collective-permute-start(bf16[2,2,32,256]{3,2,1,0:T(8,128)(2,1)S(1)} %pad_maximum_fusion.13), channel_id=1, source_target_pairs={{0,10},{1,11},{2,8},{3,9},{4,14},{5,15},{6,12},{7,13},{8,2},{9,3},... | collective-permute-start | bytes 196616 | tf_op jit(solution)/shard_map/ppermute | solution.py:555
  45.3 2.4 %collective-permute-start.17 = (bf16[2,2,32,256]{3,2,1,0:T(8,128)(2,1)S(1)}, bf16[2,2,32,256]{3,2,1,0:T(8,128)(2,1)S(1)}, u32[]{:S(2)}, u32[]{:S(2)}) collective-permute-start(bf16[2,2,32,256]{3,2,1,0:T(8,128)(2,1)S(1)} %pad_maximum_fusion.12), channel_id=1, source_target_pairs={{0,8},{1,9},{2,10},{3,11},{4,12},{5,13},{6,14},{7,15},{8,0},{9,1},... | collective-permute-start | bytes 196616 | tf_op jit(solution)/shard_map/ppermute | solution.py:555
  47.7 1.5 %collective-permute-start.15 = (bf16[2,2,32,256]{3,2,1,0:T(8,128)(2,1)S(1)}, bf16[2,2,32,256]{3,2,1,0:T(8,128)(2,1)S(1)}, u32[]{:S(2)}, u32[]{:S(2)}) collective-permute-start(bf16[2,2,32,256]{3,2,1,0:T(8,128)(2,1)S(1)} %pad_maximum_fusion.11), channel_id=1, source_target_pairs={{0,6},{1,7},{2,4},{3,5},{4,2},{5,3},{6,0},{7,1},{8,14},{9,15},{10,... | collective-permute-start | bytes 196616 | tf_op jit(solution)/shard_map/ppermute | solution.py:555
  49.3 2.9 %collective-permute-start.14 = (bf16[2,2,32,256]{3,2,1,0:T(8,128)(2,1)S(1)}, bf16[2,2,32,256]{3,2,1,0:T(8,128)(2,1)S(1)}, u32[]{:S(2)}, u32[]{:S(2)}) collective-permute-start(bf16[2,2,32,256]{3,2,1,0:T(8,128)(2,1)S(1)} %pad_maximum_fusion.10), channel_id=1, source_target_pairs={{0,4},{1,5},{2,6},{3,7},{4,0},{5,1},{6,2},{7,3},{8,12},{9,13},{10,... | collective-permute-start | bytes 196616 | tf_op jit(solution)/shard_map/ppermute | solution.py:555
  52.2 2.6 %collective-permute-done.18.refs_5_ = bf16[2,2,32,256]{3,2,1,0:T(8,128)(2,1)S(1)} collective-permute-done((bf16[2,2,32,256]{3,2,1,0:T(8,128)(2,1)S(1)}, bf16[2,2,32,256]{3,2,1,0:T(8,128)(2,1)S(1)}, u32[]{:S(2)}, u32[]{:S(2)}) %collective-permute-start.18) | collective-permute-done | bytes 65568 | tf_op jit(solution)/shard_map/ppermute | solution.py:555
  55.8 0.7 %collective-permute-done.13.refs_1_ = bf16[2,2,32,256]{3,2,1,0:T(8,128)(2,1)S(1)} collective-permute-done((bf16[2,2,32,256]{3,2,1,0:T(8,128)(2,1)S(1)}, bf16[2,2,32,256]{3,2,1,0:T(8,128)(2,1)S(1)}, u32[]{:S(2)}, u32[]{:S(2)}) %collective-permute-start.13) | collective-permute-done | bytes 65568 | tf_op jit(solution)/shard_map/ppermute | solution.py:555
  56.5 3.5 %feed.1 = bf16[32,32,256]{2,1,0:T(8,128)(2,1)} custom-call(bf16[2,2,32,256]{3,2,1,0:T(8,128)(2,1)S(1)} %pad_maximum_fusion.8.refs_0_, bf16[2,2,32,256]{3,2,1,0:T(8,128)(2,1)S(1)} %collective-permute-done.13.refs_1_, bf16[2,2,32,256]{3,2,1,0:T(8,128)(2,1)S(1)} %collective-permute-done.14.refs_2_, bf16[2,2,32,256]{3,2,1,0:T(8,128)(2,1)S(1)} %collective-permute-done.15.refs_3_, ...), custom_call_target="tpu_custom_call" | custom-call | flops 1073741824 | bytes 2000000 | tf_op jit(solution)/shard_map/feed/pallas_call | solution.py:496
  (91 shorter events, 5.7 us)
Async XLA Ops:
  1.1 1.4 %collective-permute-start = (bf16[32,256]{1,0:T(8,128)(2,1)S(1)}, bf16[32,256]{1,0:T(8,128)(2,1)S(1)}, u32[]{:S(2)}, u32[]{:S(2)}) collective-permute-start(bf16[32,256]{1,0:T(8,128)(2,1)S(1)} %border.1), channel_id=1, source_target_pairs={{0,1},{1,0},{2,3},{3,2},{4,5},{5,4},{6,7},{7,6},{8,9},{9,8},{10,11... | collective-permute-start | bytes 49160 | tf_op jit(solution)/shard_map/ppermute | solution.py:557
  2.7 5.6 %collective-permute-start.1 = (bf16[48,256]{1,0:T(8,128)(2,1)S(1)}, bf16[48,256]{1,0:T(8,128)(2,1)S(1)}, u32[]{:S(2)}, u32[]{:S(2)}) collective-permute-start(bf16[48,256]{1,0:T(8,128)(2,1)S(1)} %get-tuple-element.20), channel_id=1, source_target_pairs={{0,2},{2,0},{4,6},{6,4},{8,10},{10,8},{12,14},{14,12},{1,3},{3,1},... | collective-permute-start | bytes 73736 | tf_op jit(solution)/shard_map/ppermute | solution.py:563
  5.6 2.7 %collective-permute-start.2 = (bf16[48,256]{1,0:T(8,128)(2,1)S(1)}, bf16[48,256]{1,0:T(8,128)(2,1)S(1)}, u32[]{:S(2)}, u32[]{:S(2)}) collective-permute-start(bf16[48,256]{1,0:T(8,128)(2,1)S(1)} %get-tuple-element.21), channel_id=1, source_target_pairs={{2,4},{6,8},{10,12},{4,2},{8,6},{12,10},{3,5},{7,9},{11,13},{5,3},... | collective-permute-start | bytes 73736 | tf_op jit(solution)/shard_map/ppermute | solution.py:562
  8.8 26.4 %copy-start.7 = (bf16[256,768]{1,0:T(8,128)(2,1)S(1)}, bf16[256,768]{1,0:T(8,128)(2,1)}, u32[]{:S(2)}) copy-start(bf16[256,768]{1,0:T(8,128)(2,1)} %refs_10_.2) | copy-start | bytes 1179652
  8.8 26.4 %copy-start.8 = (bf16[256,256]{1,0:T(8,128)(2,1)S(1)}, bf16[256,256]{1,0:T(8,128)(2,1)}, u32[]{:S(2)}) copy-start(bf16[256,256]{1,0:T(8,128)(2,1)} %refs_11_.1) | copy-start | bytes 393220
  8.8 26.4 %copy-start.16 = (f32[256]{0:T(256)S(1)}, f32[256]{0:T(256)}, u32[]{:S(2)}) copy-start(f32[256]{0:T(256)} %param.29) | copy-start | bytes 3076
  14.2 1.4 %collective-permute-start.7 = (bf16[2,2,2,32,256]{4,3,2,1,0:T(8,128)(2,1)S(1)}, bf16[2,2,2,32,256]{4,3,2,1,0:T(8,128)(2,1)S(1)}, u32[]{:S(2)}, u32[]{:S(2)}) collective-permute-start(bf16[2,2,2,32,256]{4,3,2,1,0:T(8,128)(2,1)S(1)} %get-tuple-element.28), channel_id=1, source_target_pairs={{0,1},{1,0},{2,3},{3,2},{4,5},{5,4},{6,7},{7,6},{8,9},{9,8},{10,11... | collective-permute-start | bytes 393224 | tf_op jit(solution)/shard_map/ppermute | solution.py:555
  14.3 13.0 %collective-permute-start.3 = (bf16[2,2,2,32,256]{4,3,2,1,0:T(8,128)(2,1)S(1)}, bf16[2,2,2,32,256]{4,3,2,1,0:T(8,128)(2,1)S(1)}, u32[]{:S(2)}, u32[]{:S(2)}) collective-permute-start(bf16[2,2,2,32,256]{4,3,2,1,0:T(8,128)(2,1)S(1)} %get-tuple-element.26), channel_id=1, source_target_pairs={{0,1},{1,0},{2,3},{3,2},{4,5},{5,4},{6,7},{7,6},{8,9},{9,8},{10,11... | collective-permute-start | bytes 393224 | tf_op jit(solution)/shard_map/ppermute | solution.py:555
  15.6 13.2 %collective-permute-start.11 = (bf16[2,2,32,256]{3,2,1,0:T(8,128)(2,1)S(1)}, bf16[2,2,32,256]{3,2,1,0:T(8,128)(2,1)S(1)}, u32[]{:S(2)}, u32[]{:S(2)}) collective-permute-start(bf16[2,2,32,256]{3,2,1,0:T(8,128)(2,1)S(1)} %pad_maximum_fusion.7), channel_id=1, source_target_pairs={{0,14},{1,15},{2,12},{3,13},{4,10},{5,11},{6,8},{7,9},{8,6},{9,7},... | collective-permute-start | bytes 196616 | tf_op jit(solution)/shard_map/ppermute | solution.py:555
  19.9 9.6 %collective-permute-start.10 = (bf16[2,2,32,256]{3,2,1,0:T(8,128)(2,1)S(1)}, bf16[2,2,32,256]{3,2,1,0:T(8,128)(2,1)S(1)}, u32[]{:S(2)}, u32[]{:S(2)}) collective-permute-start(bf16[2,2,32,256]{3,2,1,0:T(8,128)(2,1)S(1)} %pad_maximum_fusion.6), channel_id=1, source_target_pairs={{0,12},{1,13},{2,14},{3,15},{4,8},{5,9},{6,10},{7,11},{8,4},{9,5},... | collective-permute-start | bytes 196616 | tf_op jit(solution)/shard_map/ppermute | solution.py:555
  23.3 10.7 %collective-permute-start.9 = (bf16[2,2,32,256]{3,2,1,0:T(8,128)(2,1)S(1)}, bf16[2,2,32,256]{3,2,1,0:T(8,128)(2,1)S(1)}, u32[]{:S(2)}, u32[]{:S(2)}) collective-permute-start(bf16[2,2,32,256]{3,2,1,0:T(8,128)(2,1)S(1)} %pad_maximum_fusion.5), channel_id=1, source_target_pairs={{0,10},{1,11},{2,8},{3,9},{4,14},{5,15},{6,12},{7,13},{8,2},{9,3},... | collective-permute-start | bytes 196616 | tf_op jit(solution)/shard_map/ppermute | solution.py:555
  25.3 9.5 %collective-permute-start.8 = (bf16[2,2,32,256]{3,2,1,0:T(8,128)(2,1)S(1)}, bf16[2,2,32,256]{3,2,1,0:T(8,128)(2,1)S(1)}, u32[]{:S(2)}, u32[]{:S(2)}) collective-permute-start(bf16[2,2,32,256]{3,2,1,0:T(8,128)(2,1)S(1)} %pad_maximum_fusion.4), channel_id=1, source_target_pairs={{0,8},{1,9},{2,10},{3,11},{4,12},{5,13},{6,14},{7,15},{8,0},{9,1},... | collective-permute-start | bytes 196616 | tf_op jit(solution)/shard_map/ppermute | solution.py:555
  27.3 7.5 %collective-permute-start.6 = (bf16[2,2,32,256]{3,2,1,0:T(8,128)(2,1)S(1)}, bf16[2,2,32,256]{3,2,1,0:T(8,128)(2,1)S(1)}, u32[]{:S(2)}, u32[]{:S(2)}) collective-permute-start(bf16[2,2,32,256]{3,2,1,0:T(8,128)(2,1)S(1)} %pad_maximum_fusion.3), channel_id=1, source_target_pairs={{0,6},{1,7},{2,4},{3,5},{4,2},{5,3},{6,0},{7,1},{8,14},{9,15},{10,... | collective-permute-start | bytes 196616 | tf_op jit(solution)/shard_map/ppermute | solution.py:555
  28.9 6.3 %collective-permute-start.5 = (bf16[2,2,32,256]{3,2,1,0:T(8,128)(2,1)S(1)}, bf16[2,2,32,256]{3,2,1,0:T(8,128)(2,1)S(1)}, u32[]{:S(2)}, u32[]{:S(2)}) collective-permute-start(bf16[2,2,32,256]{3,2,1,0:T(8,128)(2,1)S(1)} %pad_maximum_fusion.2), channel_id=1, source_target_pairs={{0,4},{1,5},{2,6},{3,7},{4,0},{5,1},{6,2},{7,3},{8,12},{9,13},{10,... | collective-permute-start | bytes 196616 | tf_op jit(solution)/shard_map/ppermute | solution.py:555
  29.5 5.6 %collective-permute-start.4 = (bf16[2,2,32,256]{3,2,1,0:T(8,128)(2,1)S(1)}, bf16[2,2,32,256]{3,2,1,0:T(8,128)(2,1)S(1)}, u32[]{:S(2)}, u32[]{:S(2)}) collective-permute-start(bf16[2,2,32,256]{3,2,1,0:T(8,128)(2,1)S(1)} %pad_maximum_fusion.1), channel_id=1, source_target_pairs={{0,2},{1,3},{2,0},{3,1},{4,6},{5,7},{6,4},{7,5},{8,10},{9,11},{10,... | collective-permute-start | bytes 196616 | tf_op jit(solution)/shard_map/ppermute | solution.py:555
  38.0 1.4 %collective-permute-start.16 = (bf16[2,2,2,32,256]{4,3,2,1,0:T(8,128)(2,1)S(1)}, bf16[2,2,2,32,256]{4,3,2,1,0:T(8,128)(2,1)S(1)}, u32[]{:S(2)}, u32[]{:S(2)}) collective-permute-start(bf16[2,2,2,32,256]{4,3,2,1,0:T(8,128)(2,1)S(1)} %get-tuple-element.32), channel_id=1, source_target_pairs={{0,1},{1,0},{2,3},{3,2},{4,5},{5,4},{6,7},{7,6},{8,9},{9,8},{10,11... | collective-permute-start | bytes 393224 | tf_op jit(solution)/shard_map/ppermute | solution.py:555
  38.1 9.6 %collective-permute-start.12 = (bf16[2,2,2,32,256]{4,3,2,1,0:T(8,128)(2,1)S(1)}, bf16[2,2,2,32,256]{4,3,2,1,0:T(8,128)(2,1)S(1)}, u32[]{:S(2)}, u32[]{:S(2)}) collective-permute-start(bf16[2,2,2,32,256]{4,3,2,1,0:T(8,128)(2,1)S(1)} %get-tuple-element.30), channel_id=1, source_target_pairs={{0,1},{1,0},{2,3},{3,2},{4,5},{5,4},{6,7},{7,6},{8,9},{9,8},{10,11... | collective-permute-start | bytes 393224 | tf_op jit(solution)/shard_map/ppermute | solution.py:555
  39.4 9.8 %collective-permute-start.20 = (bf16[2,2,32,256]{3,2,1,0:T(8,128)(2,1)S(1)}, bf16[2,2,32,256]{3,2,1,0:T(8,128)(2,1)S(1)}, u32[]{:S(2)}, u32[]{:S(2)}) collective-permute-start(bf16[2,2,32,256]{3,2,1,0:T(8,128)(2,1)S(1)} %pad_maximum_fusion.15), channel_id=1, source_target_pairs={{0,14},{1,15},{2,12},{3,13},{4,10},{5,11},{6,8},{7,9},{8,6},{9,7},... | collective-permute-start | bytes 196616 | tf_op jit(solution)/shard_map/ppermute | solution.py:555
  43.6 8.6 %collective-permute-start.19 = (bf16[2,2,32,256]{3,2,1,0:T(8,128)(2,1)S(1)}, bf16[2,2,32,256]{3,2,1,0:T(8,128)(2,1)S(1)}, u32[]{:S(2)}, u32[]{:S(2)}) collective-permute-start(bf16[2,2,32,256]{3,2,1,0:T(8,128)(2,1)S(1)} %pad_maximum_fusion.14), channel_id=1, source_target_pairs={{0,12},{1,13},{2,14},{3,15},{4,8},{5,9},{6,10},{7,11},{8,4},{9,5},... | collective-permute-start | bytes 196616 | tf_op jit(solution)/shard_map/ppermute | solution.py:555
  43.7 11.2 %collective-permute-start.18 = (bf16[2,2,32,256]{3,2,1,0:T(8,128)(2,1)S(1)}, bf16[2,2,32,256]{3,2,1,0:T(8,128)(2,1)S(1)}, u32[]{:S(2)}, u32[]{:S(2)}) collective-permute-start(bf16[2,2,32,256]{3,2,1,0:T(8,128)(2,1)S(1)} %pad_maximum_fusion.13), channel_id=1, source_target_pairs={{0,10},{1,11},{2,8},{3,9},{4,14},{5,15},{6,12},{7,13},{8,2},{9,3},... | collective-permute-start | bytes 196616 | tf_op jit(solution)/shard_map/ppermute | solution.py:555
  45.3 9.9 %collective-permute-start.17 = (bf16[2,2,32,256]{3,2,1,0:T(8,128)(2,1)S(1)}, bf16[2,2,32,256]{3,2,1,0:T(8,128)(2,1)S(1)}, u32[]{:S(2)}, u32[]{:S(2)}) collective-permute-start(bf16[2,2,32,256]{3,2,1,0:T(8,128)(2,1)S(1)} %pad_maximum_fusion.12), channel_id=1, source_target_pairs={{0,8},{1,9},{2,10},{3,11},{4,12},{5,13},{6,14},{7,15},{8,0},{9,1},... | collective-permute-start | bytes 196616 | tf_op jit(solution)/shard_map/ppermute | solution.py:555
  47.7 7.5 %collective-permute-start.15 = (bf16[2,2,32,256]{3,2,1,0:T(8,128)(2,1)S(1)}, bf16[2,2,32,256]{3,2,1,0:T(8,128)(2,1)S(1)}, u32[]{:S(2)}, u32[]{:S(2)}) collective-permute-start(bf16[2,2,32,256]{3,2,1,0:T(8,128)(2,1)S(1)} %pad_maximum_fusion.11), channel_id=1, source_target_pairs={{0,6},{1,7},{2,4},{3,5},{4,2},{5,3},{6,0},{7,1},{8,14},{9,15},{10,... | collective-permute-start | bytes 196616 | tf_op jit(solution)/shard_map/ppermute | solution.py:555
  49.3 6.5 %collective-permute-start.14 = (bf16[2,2,32,256]{3,2,1,0:T(8,128)(2,1)S(1)}, bf16[2,2,32,256]{3,2,1,0:T(8,128)(2,1)S(1)}, u32[]{:S(2)}, u32[]{:S(2)}) collective-permute-start(bf16[2,2,32,256]{3,2,1,0:T(8,128)(2,1)S(1)} %pad_maximum_fusion.10), channel_id=1, source_target_pairs={{0,4},{1,5},{2,6},{3,7},{4,0},{5,1},{6,2},{7,3},{8,12},{9,13},{10,... | collective-permute-start | bytes 196616 | tf_op jit(solution)/shard_map/ppermute | solution.py:555
  52.2 4.3 %collective-permute-start.13 = (bf16[2,2,32,256]{3,2,1,0:T(8,128)(2,1)S(1)}, bf16[2,2,32,256]{3,2,1,0:T(8,128)(2,1)S(1)}, u32[]{:S(2)}, u32[]{:S(2)}) collective-permute-start(bf16[2,2,32,256]{3,2,1,0:T(8,128)(2,1)S(1)} %pad_maximum_fusion.9), channel_id=1, source_target_pairs={{0,2},{1,3},{2,0},{3,1},{4,6},{5,7},{6,4},{7,5},{8,10},{9,11},{10,... | collective-permute-start | bytes 196616 | tf_op jit(solution)/shard_map/ppermute | solution.py:555
  (18 other events, 219.3 us)
